TPU v7x, 32 devices: a whole 2x2x4 slice. The times are simulated.
32 devices in a mesh: expert: 8 (over z, y), tensor: 4 (over x, core).
Axes of the slice: x: 2, y: 2, z: 4, core: 2. Of those that a mesh axis runs over, the one named last changes fastest.
Arguments:
- tokens: bfloat16 [1024, 8192], P('expert', 'tensor'), may hold values from -25 to 25, as said below
- routes: int32 [1024, 2], P('expert'), may hold values from 0 to 7, all different within a row; in each aligned block of 128 rows (0 to 127, 128 to 255, ...) at most 48 rows name the same one
- norm_gain: float32 [2, 8192], P(None, 'tensor'), may hold values from 0.5 to 1.5
- router_weight: bfloat16 [2, 8192, 8], P(None, 'tensor'), may hold values from -0.0625 to 0.0625
- gate_codes: int32 [2, 8, 4096, 1024], P(None, 'expert', None, 'tensor'), may hold values from 0 to 255
- gate_scales: int32 [2, 8, 64, 1024], P(None, 'expert', None, 'tensor'), may hold values from 8 to 10
- up_codes: int32 [2, 8, 4096, 1024], P(None, 'expert', None, 'tensor'), may hold values from 0 to 255
- up_scales: int32 [2, 8, 64, 1024], P(None, 'expert', None, 'tensor'), may hold values from 8 to 10
- down_codes: int32 [2, 8, 512, 8192], P(None, 'expert', 'tensor'), may hold values from 0 to 255
- down_scales: int32 [2, 8, 8, 8192], P(None, 'expert', 'tensor'), may hold values from 6 to 8
Outputs:
- hidden_out: bfloat16 [1024, 8192], P('expert', 'tensor')
Inputs may be any that keep to these rules, and one draw needn't show every extreme that they name: `routes`: in the rows of one index of expert (128 aligned rows) no expert is named by more than 48 rows, a bound that some block reaches; the two experts of a row differ. `tokens`: token activations.
All inputs are finite; a program needn't handle non-finite values.
Results may differ from a plain program's by a relative error of at most 0.029.
Values may be sent and summed in bfloat16 or wider, within the bound.
No kernel may reach another device: no remote copies, remote signals or barrier semaphores. Data moves between devices by JAX's collectives and lax.ppermute only.
A program may use at most 192 MiB of HBM per device.

v0:
```python
import math

import jax
import jax.numpy as jnp
import numpy as np
from jax import lax
from jax.sharding import PartitionSpec as P

LAYERS = 2


def from_partner(shard, axis, stride):
    return lax.ppermute(shard, axis, [(i, i ^ 1 << stride) for i in range(lax.axis_size(axis))])


def hadamard(table_order):
    matrix = np.ones((1, 1), np.float32)
    for repeat_idx in range(table_order.bit_length() - 1):
        matrix = np.kron(np.array([[1.0, 1.0], [1.0, -1.0]], np.float32), matrix)
    return matrix


def unpack(words):
    shifts = jnp.arange(2, dtype=jnp.int32) * 4
    nibbles = jnp.bitwise_and(jnp.right_shift(words[:, None, :], shifts[None, :, None]), 15) - 8
    return nibbles.reshape(words.shape[0] * 2, words.shape[1])


def dequant(words, scales):
    codes = unpack(words)
    groups = scales.shape[0]
    shaped = codes.reshape(groups, codes.shape[0] // groups, codes.shape[1]).astype(jnp.float32)
    factor = jnp.exp2(-scales.astype(jnp.float32))
    return (shaped * factor[:, None, :]).reshape(codes.shape).astype(jnp.bfloat16)


def rotate_local(matrix_rows, first_table, second_table):
    row_count = matrix_rows.shape[0]
    first_order = first_table.shape[0]
    second_order = second_table.shape[0]
    shaped = matrix_rows.reshape(row_count, first_order, second_order)
    section_one = jnp.einsum(
        "rab,bc->rac", shaped, second_table, preferred_element_type=jnp.float32
    )
    section_two = jnp.einsum(
        "rac,ad->rdc", section_one, first_table, precision=lax.Precision.HIGHEST
    )
    return section_two.reshape(row_count, first_order * second_order)


def rotate_butterfly(normed, first_table, second_table, parts_count):
    partial_value = rotate_local(normed, first_table, second_table)
    tensor_index = lax.axis_index("tensor")
    for bit_pos in range(parts_count.bit_length() - 1):
        partner = from_partner(partial_value.astype(jnp.bfloat16), "tensor", bit_pos).astype(
            partial_value.dtype
        )
        upper = tensor_index >> bit_pos & 1 == 1
        partial_value = jnp.where(upper, partner - partial_value, partial_value + partner)
    full_width = parts_count * normed.shape[1]
    return (partial_value * (1.0 / math.sqrt(full_width))).astype(jnp.bfloat16)


def expert_activation(inputs, gate_w, up_w):
    gate_out = jnp.dot(inputs, gate_w, preferred_element_type=jnp.float32)
    up_out = jnp.dot(inputs, up_w, preferred_element_type=jnp.float32)
    return (jax.nn.silu(gate_out) * up_out).astype(jnp.bfloat16)


def per_device(
    tokens,
    routes,
    norm_gain,
    router_weight,
    gate_codes,
    gate_scales,
    up_codes,
    up_scales,
    down_codes,
    down_scales,
):
    parts_count = lax.axis_size("tensor")
    expert_count = lax.axis_size("expert")
    tok_count = tokens.shape[0]
    local_width = tokens.shape[1]
    full_width = local_width * parts_count
    capacity = 3 * tok_count // expert_count
    slot_total = expert_count * capacity
    first_order = 1 << (local_width.bit_length() - 1) // 2
    second_order = local_width // first_order
    first_table = jnp.asarray(hadamard(first_order), jnp.float32)
    second_table = jnp.asarray(hadamard(second_order), jnp.bfloat16)
    flat_routes = routes.reshape(-1)
    expert_ids = jnp.arange(expert_count, dtype=jnp.int32)
    onehot = (flat_routes[:, None] == expert_ids[None, :]).astype(jnp.int32)
    earlier = jnp.cumsum(onehot, axis=0) - onehot
    ranks = jnp.sum(earlier * onehot, axis=1)
    slot_ids = flat_routes * capacity + ranks
    token_of = jnp.arange(2 * tok_count, dtype=jnp.int32) // 2
    matches = (slot_ids[None, :] == jnp.arange(slot_total, dtype=jnp.int32)[:, None]).astype(
        jnp.int32
    )
    slot_token = jnp.sum(matches * token_of[None, :], axis=1)
    slot_valid = jnp.sum(matches, axis=1) > 0
    first_slot = slot_ids[0::2]
    second_slot = slot_ids[1::2]
    first_pick = (routes[:, 0:1] == expert_ids[None, :]).astype(jnp.float32)
    second_pick = (routes[:, 1:2] == expert_ids[None, :]).astype(jnp.float32)
    stream = tokens.astype(jnp.float32)
    for layer_idx in range(LAYERS):
        square = lax.psum(jnp.sum(stream * stream, axis=1), "tensor")
        normed = (
            stream * lax.rsqrt(square / full_width + 1e-05)[:, None] * norm_gain[layer_idx][None, :]
        ).astype(jnp.bfloat16)
        logits = lax.psum(
            jnp.dot(normed, router_weight[layer_idx], preferred_element_type=jnp.float32), "tensor"
        )
        first_logit = jnp.sum(logits * first_pick, axis=1)
        second_logit = jnp.sum(logits * second_pick, axis=1)
        first_weight = jax.nn.sigmoid(first_logit - second_logit)
        moving = rotate_butterfly(normed, first_table, second_table, parts_count)
        gate_w = dequant(gate_codes[layer_idx, 0], gate_scales[layer_idx, 0])
        up_w = dequant(up_codes[layer_idx, 0], up_scales[layer_idx, 0])
        down_w = dequant(down_codes[layer_idx, 0], down_scales[layer_idx, 0])
        whole = lax.all_gather(moving, "tensor", axis=1, tiled=True)
        outgoing = jnp.where(
            slot_valid[:, None], jnp.take(whole, slot_token, axis=0), jnp.zeros((), jnp.bfloat16)
        )
        slot_inputs = lax.all_to_all(outgoing, "expert", split_axis=0, concat_axis=0, tiled=True)
        activ = expert_activation(slot_inputs, gate_w, up_w)
        partial_value = jnp.dot(activ, down_w, preferred_element_type=jnp.float32)
        reduced = lax.psum_scatter(
            partial_value.astype(jnp.bfloat16), "tensor", scatter_dimension=1, tiled=True
        )
        expert_out = lax.all_to_all(reduced, "expert", split_axis=0, concat_axis=0, tiled=True)
        first_rows = jnp.take(expert_out, first_slot, axis=0).astype(jnp.float32)
        second_rows = jnp.take(expert_out, second_slot, axis=0).astype(jnp.float32)
        stream = (
            stream
            + first_weight[:, None] * first_rows
            + (1.0 - first_weight)[:, None] * second_rows
        )
    return stream.astype(jnp.bfloat16)


def solution(mesh):
    in_specs = (
        P("expert", "tensor"),
        P("expert", None),
        P(None, "tensor"),
        P(None, "tensor", None),
        P(None, "expert", None, "tensor"),
        P(None, "expert", None, "tensor"),
        P(None, "expert", None, "tensor"),
        P(None, "expert", None, "tensor"),
        P(None, "expert", "tensor", None),
        P(None, "expert", "tensor", None),
    )
    out_specs = P("expert", "tensor")
    return jax.shard_map(
        per_device, mesh=mesh, in_specs=in_specs, out_specs=out_specs, check_vma=False
    )
```

profile of v0, /device:TPU:0, one launch (start us, length us, event | category | flops | bytes accessed | tf_op | source)
XLA Modules:
  0.0 710.5 jit_solution(15770011931566689314)
XLA Ops:
  7.8 8.3 %psum.28 = f32[128]{0:T(128)S(1)} all-reduce(f32[128]{0:T(128)S(1)} %fusion.12), channel_id=1, replica_groups=mesh['expert'=8,'tensor'=4] {'tensor'}, use_global_device_ids=true, to_apply=%region_1.2 | all-reduce | flops 128 | bytes 1024 | tf_op jit(solution)/shard_map/psum | solution.py:111
  19.5 2.4 convolution_bitcast_fusion.1
  23.0 1.9 collective-permute-done
  25.5 13.6 %collective-permute-done.1 = bf16[128,2048]{1,0:T(8,128)(2,1)S(1)} collective-permute-done((bf16[128,2048]{1,0:T(8,128)(2,1)S(1)}, bf16[128,2048]{1,0:T(8,128)(2,1)S(1)}, u32[]{:S(2)}, u32[]{:S(2)}) %collective-permute-start.1) | collective-permute-done | bytes 524320 | tf_op jit(solution)/shard_map/ppermute | solution.py:13
  41.8 21.4 %all-gather.3.cloned.1.call-done = bf16[128,8192]{1,0:T(8,128)(2,1)} async-done(((bf16[128,2048]{1,0:T(8,128)(2,1)}), bf16[128,8192]{1,0:T(8,128)(2,1)}) %all-gather.3.cloned.1.call-update) | async-done | bytes 2097168 | tf_op jit(solution)/shard_map/all_gather | solution.py:125
  63.3 16.9 %gather_fusion = bf16[384,8192]{1,0:T(8,128)(2,1)} fusion(bf16[128,8192]{1,0:T(8,128)(2,1)} %all-gather.3.cloned.1.call-done, s32[1024]{0:T(1024)S(1)} %pad_clamp_fusion.2), kind=kCustom, calls=%fused_computation.clone | custom fusion | bytes 12584448 | tf_op jit(solution)/shard_map/jit(_take)/gather | solution.py:127
  80.1 6.1 select_select_fusion.1
  86.3 5.5 all-to-all-start
  92.0 6.0 slice_bitcast_fusion.2
  98.0 4.6 shift_right_arithmetic.203
  102.6 10.9 %shift_right_arithmetic.204 = s32[64,128,256]{2,1,0:T(8,128)} reshape(s32[4096,2,256]{2,1,0:T(2,128)} %shift_right_arithmetic.203) | data formatting | bytes 16777216 | tf_op jit(solution)/shard_map/shift_right_arithmetic | solution.py:25
  113.4 6.6 shift_right_arithmetic.185
  120.1 10.9 %shift_right_arithmetic.186 = s32[64,128,256]{2,1,0:T(8,128)} reshape(s32[4096,2,256]{2,1,0:T(2,128)} %shift_right_arithmetic.185) | data formatting | bytes 16777216 | tf_op jit(solution)/shard_map/shift_right_arithmetic | solution.py:25
  130.9 5.9 slice_bitcast_fusion.1
  136.9 4.6 shift_right_arithmetic.207
  141.4 10.9 %shift_right_arithmetic.208 = s32[64,128,256]{2,1,0:T(8,128)} reshape(s32[4096,2,256]{2,1,0:T(2,128)} %shift_right_arithmetic.207) | data formatting | bytes 16777216 | tf_op jit(solution)/shard_map/shift_right_arithmetic | solution.py:25
  152.3 6.6 shift_right_arithmetic.192
  158.9 10.9 %shift_right_arithmetic.193 = s32[64,128,256]{2,1,0:T(8,128)} reshape(s32[4096,2,256]{2,1,0:T(2,128)} %shift_right_arithmetic.192) | data formatting | bytes 16777216 | tf_op jit(solution)/shard_map/shift_right_arithmetic | solution.py:25
  169.8 6.1 slice_bitcast_fusion
  175.9 5.3 shift_right_arithmetic.211
  181.3 10.9 %shift_right_arithmetic.212 = s32[256,8192]{1,0:T(8,128)} reshape(s32[128,2,8192]{2,1,0:T(2,128)} %shift_right_arithmetic.211) | data formatting | bytes 16777216 | tf_op jit(solution)/shard_map/shift_right_arithmetic | solution.py:25
  192.2 7.1 %shift_right_arithmetic.196 = s32[128,2,8192]{2,1,0:T(2,128)} broadcast(s32[128,8192]{1,0:T(8,128)} %get-tuple-element.24), dimensions={0,2} | broadcast | bytes 12582912 | tf_op jit(solution)/shard_map/shift_right_arithmetic | solution.py:25
  199.3 10.9 %shift_right_arithmetic.197 = s32[256,8192]{1,0:T(8,128)} reshape(s32[128,2,8192]{2,1,0:T(2,128)} %shift_right_arithmetic.196) | data formatting | bytes 16777216 | tf_op jit(solution)/shard_map/shift_right_arithmetic | solution.py:25
  210.3 9.6 %fusion = (bf16[256,8192]{1,0:T(8,128)(2,1)}, bf16[256,8192]{1,0:T(8,128)(2,1)}) fusion(s32[256,8192]{1,0:T(8,128)} %shift_right_arithmetic.212, f32[2,8192]{1,0:T(2,128)S(1)} %get-tuple-element.29, s32[256]{0:T(256)S(1)} %broadcast_bitcast_fusion, f32[2,8192]{1,0:T(2,128)S(1)} %get-tuple-element.30, s32[256,8192]{1,0:T(8,128)} %shift_right_arithmetic.197), kind=kLoop, calls=%fused_computation.9 | loop fusion | flops 25165824 | bytes 25297920 | tf_op jit(solution)/shard_map/convert_element_type | solution.py:34
  219.9 20.1 %multiply_convert_fusion.1 = (bf16[64,128,256]{2,1,0:T(8,128)(2,1)}, bf16[64,128,256]{2,1,0:T(8,128)(2,1)}, bf16[64,128,256]{2,1,0:T(8,128)(2,1)}, bf16[64,128,256]{2,1,0:T(8,128)(2,1)}) fusion(s32[64,128,256]{2,1,0:T(8,128)} %shift_right_arithmetic.204, f32[64,256]{1,0:T(8,128)S(1)} %get-tuple-element.44, s32[128]{0:T(128)S(1)} %shift_right_arithmetic.188, ...), kind=kLoop, calls=%fused_computation.13 | loop fusion | flops 50331648 | bytes 50594304 | tf_op jit(solution)/shard_map/convert_element_type | solution.py:34
  240.0 5.8 fusion.45
  245.8 14.6 %convolution_convert_fusion.1 = bf16[384,8192]{1,0:T(8,128)(2,1)} fusion(bf16[256,8192]{1,0:T(8,128)(2,1)} %get-tuple-element.34, bf16[384,8192]{1,0:T(8,128)(2,1)} %bitcast.12, bf16[8192,256]{1,0:T(8,128)(2,1)} %bitcast.95, f32[384,256]{1,0:T(8,128)S(1)} %fusion.45), kind=kOutput, calls=%fused_computation.7 | convolution fusion | flops 3224961024 | bytes 21364736 | tf_op jit(solution)/shard_map/dot_general | solution.py:131
  260.4 59.0 %reduce-scatter.3.cloned.1.call-done = bf16[384,2048]{1,0:T(8,128)(2,1)} async-done(((bf16[384,8192]{1,0:T(8,128)(2,1)}), bf16[384,2048]{1,0:T(8,128)(2,1)}) %reduce-scatter.3.cloned.1.call-update) | async-done | bytes 1572880 | tf_op jit(solution)/shard_map/reduce_scatter | solution.py:132
  319.4 5.6 all-to-all-start.1
  325.8 6.1 psum.29
  332.0 30.0 %all-to-all-done.1 = bf16[8,48,2048]{2,1,0:T(8,128)(2,1)S(1)} async-done(((bf16[8,48,2048]{2,1,0:T(8,128)(2,1)}), bf16[8,48,2048]{2,1,0:T(8,128)(2,1)S(1)}, u32[]{:S(2)}, u32[]{:S(2)}) %all-to-all-start.1) | async-done | bytes 1572896 | tf_op jit(solution)/shard_map/all_to_all | solution.py:135
  363.8 1.7 gather_fusion.1
  365.5 1.7 multiply_reduce_fusion
  367.2 6.0 psum.30
  378.9 1.9 collective-permute-done.2
  381.3 13.7 %collective-permute-done.3 = bf16[128,2048]{1,0:T(8,128)(2,1)S(1)} collective-permute-done((bf16[128,2048]{1,0:T(8,128)(2,1)S(1)}, bf16[128,2048]{1,0:T(8,128)(2,1)S(1)}, u32[]{:S(2)}, u32[]{:S(2)}) %collective-permute-start.3) | collective-permute-done | bytes 524320 | tf_op jit(solution)/shard_map/ppermute | solution.py:13
  396.2 21.7 %all-gather.5.cloned.1.call-done = bf16[128,8192]{1,0:T(8,128)(2,1)} async-done(((bf16[128,2048]{1,0:T(8,128)(2,1)}), bf16[128,8192]{1,0:T(8,128)(2,1)}) %all-gather.5.cloned.1.call-update) | async-done | bytes 2097168 | tf_op jit(solution)/shard_map/all_gather | solution.py:125
  417.9 16.7 %gather_fusion.3 = bf16[384,8192]{1,0:T(8,128)(2,1)} fusion(bf16[128,8192]{1,0:T(8,128)(2,1)} %all-gather.5.cloned.1.call-done, s32[1024]{0:T(1024)S(1)} %pad_clamp_fusion.2), kind=kCustom, calls=%fused_computation.2.clone | custom fusion | bytes 12584448 | tf_op jit(solution)/shard_map/jit(_take)/gather | solution.py:127
  434.6 3.5 select_select_fusion
  438.2 144.3 %all_to_all.48 = bf16[8,48,8192]{2,1,0:T(8,128)(2,1)S(1)} all-to-all(bf16[8,48,8192]{2,1,0:T(8,128)(2,1)S(1)} %bitcast.103), channel_id=1, replica_groups=mesh['expert'=8,'tensor'=4] {'expert'}, dimensions={0} | all-to-all | bytes 12582912 | tf_op jit(solution)/shard_map/all_to_all | solution.py:129
  582.4 1.8 fusion.46
  585.1 14.6 %convolution_convert_fusion = bf16[384,8192]{1,0:T(8,128)(2,1)} fusion(bf16[256,8192]{1,0:T(8,128)(2,1)} %get-tuple-element.33, bf16[384,8192]{1,0:T(8,128)(2,1)} %bitcast.102, bf16[8192,256]{1,0:T(8,128)(2,1)} %bitcast.94, f32[384,256]{1,0:T(8,128)S(1)} %fusion.46), kind=kOutput, calls=%fused_computation.6 | convolution fusion | flops 3224961024 | bytes 21364736 | tf_op jit(solution)/shard_map/dot_general | solution.py:131
  599.7 56.7 %reduce-scatter.5.cloned.1.call-done = bf16[384,2048]{1,0:T(8,128)(2,1)} async-done(((bf16[384,8192]{1,0:T(8,128)(2,1)}), bf16[384,2048]{1,0:T(8,128)(2,1)}) %reduce-scatter.5.cloned.1.call-update) | async-done | bytes 1572880 | tf_op jit(solution)/shard_map/reduce_scatter | solution.py:132
  656.3 5.5 all-to-all-start.3
  662.1 6.0 psum.31
  668.1 30.8 %all-to-all-done.3 = bf16[8,48,2048]{2,1,0:T(8,128)(2,1)S(1)} async-done(((bf16[8,48,2048]{2,1,0:T(8,128)(2,1)}), bf16[8,48,2048]{2,1,0:T(8,128)(2,1)S(1)}, u32[]{:S(2)}, u32[]{:S(2)}) %all-to-all-start.3) | async-done | bytes 1572896 | tf_op jit(solution)/shard_map/all_to_all | solution.py:135
  699.8 1.7 gather_fusion.4
  701.5 2.2 add_convert_fusion
  (91 shorter events, 21.2 us)
Async XLA Ops:
  6.5 56.7 %all-gather.3.cloned.1.call-start = ((), (), s32[]{:S(2)}) async-start(), calls=%async_computation.6 | async-start | bytes 2621440 | tf_op jit(solution)/shard_map/all_gather | solution.py:125
  19.4 20.8 %copy-start.9 = (s32[128,2]{0,1:T(2,128)S(1)}, s32[128,2]{0,1:T(2,128)}, u32[]{:S(2)}) copy-start(s32[128,2]{0,1:T(2,128)} %param.17) | copy-start | bytes 3076
  22.9 2.0 collective-permute-start
  25.0 14.0 %collective-permute-start.1 = (bf16[128,2048]{1,0:T(8,128)(2,1)S(1)}, bf16[128,2048]{1,0:T(8,128)(2,1)S(1)}, u32[]{:S(2)}, u32[]{:S(2)}) collective-permute-start(bf16[128,2048]{1,0:T(8,128)(2,1)S(1)} %fusion.19), channel_id=1, source_target_pairs={{0,2},{1,3},{2,0},{3,1},{4,6},{5,7},{6,4},{7,5},{8,10},{9,11},{10,... | collective-permute-start | bytes 1572872 | tf_op jit(solution)/shard_map/ppermute | solution.py:13
  86.3 153.7 %all-to-all-start = ((bf16[8,48,8192]{2,1,0:T(8,128)(2,1)}), bf16[8,48,8192]{2,1,0:T(8,128)(2,1)}, u32[]{:S(2)}, u32[]{:S(2)}) async-start(bf16[8,48,8192]{2,1,0:T(8,128)(2,1)} %bitcast.100), calls=%async_computation | async-start | bytes 12582912 | tf_op jit(solution)/shard_map/all_to_all | solution.py:129
  91.8 227.6 %reduce-scatter.3.cloned.1.call-start = ((), (), s32[]{:S(2)}) async-start(), calls=%async_computation.7 | async-start | bytes 7864320 | tf_op jit(solution)/shard_map/reduce_scatter | solution.py:132
  199.3 10.9 %copy-start.3 = (s32[2,1,2,8192]{3,2,1,0:T(2,128)S(1)}, s32[2,1,2,8192]{3,2,1,0:T(2,128)}, u32[]{:S(2)}) copy-start(s32[2,1,2,8192]{3,2,1,0:T(2,128)} %param.25) | copy-start | bytes 393220
  210.3 9.6 %copy-start.4 = (s32[2,1,64,256]{3,2,1,0:T(8,128)S(1)}, s32[2,1,64,256]{3,2,1,0:T(8,128)}, u32[]{:S(2)}) copy-start(s32[2,1,64,256]{3,2,1,0:T(8,128)} %param.23) | copy-start | bytes 393220
  210.3 9.6 %copy-start.5 = (s32[2,1,64,256]{3,2,1,0:T(8,128)S(1)}, s32[2,1,64,256]{3,2,1,0:T(8,128)}, u32[]{:S(2)}) copy-start(s32[2,1,64,256]{3,2,1,0:T(8,128)} %param.21) | copy-start | bytes 393220
  260.4 65.1 %copy-start.8 = (bf16[2,2048,8]{1,2,0:T(8,128)(2,1)S(1)}, bf16[2,2048,8]{1,2,0:T(8,128)(2,1)}, u32[]{:S(2)}) copy-start(bf16[2,2048,8]{1,2,0:T(8,128)(2,1)} %param.19) | copy-start | bytes 196612
  319.4 46.1 %copy-start.1 = (bf16[128,2048]{1,0:T(8,128)(2,1)S(1)}, bf16[128,2048]{1,0:T(8,128)(2,1)}, u32[]{:S(2)}) copy-start(bf16[128,2048]{1,0:T(8,128)(2,1)} %param.16) | copy-start | bytes 1572868
  319.4 42.6 %all-to-all-start.1 = ((bf16[8,48,2048]{2,1,0:T(8,128)(2,1)}), bf16[8,48,2048]{2,1,0:T(8,128)(2,1)S(1)}, u32[]{:S(2)}, u32[]{:S(2)}) async-start(bf16[8,48,2048]{2,1,0:T(8,128)(2,1)} %bitcast.110), calls=%async_computation.2 | async-start | bytes 3145728 | tf_op jit(solution)/shard_map/all_to_all | solution.py:135
  325.0 92.9 %all-gather.5.cloned.1.call-start = ((), (), s32[]{:S(2)}) async-start(), calls=%async_computation.8 | async-start | bytes 2621440 | tf_op jit(solution)/shard_map/all_gather | solution.py:125
  362.0 11.6 %copy-start.6 = (bf16[64,64,1]{0,1,2:T(8,128)(2,1)S(1)}, bf16[64,64,1]{0,1,2:T(8,128)(2,1)}, u32[]{:S(2)}) copy-start(bf16[64,64,1]{0,1,2:T(8,128)(2,1)} %constant.100) | copy-start | bytes 24580
  363.8 10.2 %copy-start.7 = (f32[32,32,1]{0,1,2:T(8,128)S(1)}, f32[32,32,1]{0,1,2:T(8,128)}, u32[]{:S(2)}) copy-start(f32[32,32,1]{0,1,2:T(8,128)} %constant.101) | copy-start | bytes 12292
  378.8 2.0 collective-permute-start.2
  381.0 14.0 %collective-permute-start.3 = (bf16[128,2048]{1,0:T(8,128)(2,1)S(1)}, bf16[128,2048]{1,0:T(8,128)(2,1)S(1)}, u32[]{:S(2)}, u32[]{:S(2)}) collective-permute-start(bf16[128,2048]{1,0:T(8,128)(2,1)S(1)} %fusion.18), channel_id=1, source_target_pairs={{0,2},{1,3},{2,0},{3,1},{4,6},{5,7},{6,4},{7,5},{8,10},{9,11},{10,... | collective-permute-start | bytes 1572872 | tf_op jit(solution)/shard_map/ppermute | solution.py:13
  396.1 260.2 %reduce-scatter.5.cloned.1.call-start = ((), (), s32[]{:S(2)}) async-start(), calls=%async_computation.9 | async-start | bytes 7864320 | tf_op jit(solution)/shard_map/reduce_scatter | solution.py:132
  438.1 144.3 %copy-start.2 = (bf16[64,128,256]{2,1,0:T(8,128)(2,1)S(1)}, bf16[64,128,256]{2,1,0:T(8,128)(2,1)}, u32[]{:S(2)}) copy-start(bf16[64,128,256]{2,1,0:T(8,128)(2,1)} %get-tuple-element.37) | copy-start | bytes 12582916
  582.4 2.7 copy-start
  656.3 42.5 %all-to-all-start.3 = ((bf16[8,48,2048]{2,1,0:T(8,128)(2,1)}), bf16[8,48,2048]{2,1,0:T(8,128)(2,1)S(1)}, u32[]{:S(2)}, u32[]{:S(2)}) async-start(bf16[8,48,2048]{2,1,0:T(8,128)(2,1)} %bitcast.111), calls=%async_computation.5 | async-start | bytes 3145728 | tf_op jit(solution)/shard_map/all_to_all | solution.py:135
Sparse Core Ops, SparseCore 0:
  40.3 22.8 all-gather.2
  260.5 58.7 reduce-scatter.2
  396.3 21.5 all-gather.4
  599.8 56.4 reduce-scatter.4
where the time goes:
time: 722 us; the launch traced here: 711 us
  waiting for transfers between devices  251 us (35%)
  blocking collectives  171 us (24%)
  local copies, waits for them, and re-layouts  165 us (23%)
  other arithmetic  49.8 us (7%)
  matrix products  42.6 us (6%)
  starting transfers between devices  17.7 us (2%)
  between operations  13.7 us (2%)
    all_to_all x1, blocking collectives, per_device(): lax.all_to_all(outgoing, 'expert', split_axis=0, concat_axis=0, tiled=True)  144 us
    shift_right_arithmetic x18, local copies, waits for them, and re-layouts, unpack(): jnp.right_shift(words[:, None, :], shifts[None, :, None])  118 us
    reduce_scatter x2, waiting for transfers between devices, per_device(): lax.psum_scatter(partial_value.astype(jnp.bfloat16), 'tensor', scatter_di...  116 us
    all_to_all x2, waiting for transfers between devices, per_device(): lax.all_to_all(reduced, 'expert', split_axis=0, concat_axis=0, tiled=True)  60.8 us
    all_gather x2, waiting for transfers between devices, per_device(): whole = lax.all_gather(moving, 'tensor', axis=1, tiled=True)  43.1 us
    gather x2, local copies, waits for them, and re-layouts, per_device(): jnp.take(whole, slot_token, axis=0)  33.6 us
    ppermute x4, waiting for transfers between devices, from_partner(): lax.ppermute(shard, axis, [(i, i ^ 1 << stride) for i in range(lax.axis_s...  31.1 us
    convert_element_type x2, other arithmetic, dequant(): (shaped * factor[:, None, :]).reshape(codes.shape).astype(jnp.bfloat16)  29.6 us
  transfers between devices with their start and end apart: 11, of which 10 were waited for; matrix products, arithmetic and copies ran while one was open for 21% of the time, Pallas kernels for 0%

commit v1 on v0

v1 whole, which is shorter than its diff:
```python
import functools
import math

import jax
import jax.numpy as jnp
import numpy as np
from jax import lax
from jax.experimental import pallas as pl
from jax.experimental.pallas import tpu as pltpu
from jax.sharding import PartitionSpec as P

LAYERS = 2
GROUP = 128
BLOCK = 256
MIB = 1 << 20
FIRST = 4
SECOND = 32
NT = (((1,), (1,)), ((), ()))
TN = (((0,), (0,)), ((), ()))


def exchange(shard, axis, mask):
    return lax.ppermute(shard, axis, [(i, i ^ mask) for i in range(lax.axis_size(axis))])


def block_table():
    index = np.arange(BLOCK)
    order = np.concatenate([index[0::2], index[1::2]])
    common = index[:, None] & order[None, :]
    ones = np.array([bin(v).count("1") for v in range(BLOCK)])[common]
    return np.where(ones % 2 == 1, -1.0, 1.0).astype(np.float32)


def split_table(width):
    table = np.zeros((width, width), np.float32)
    for unit in range(width):
        table[unit, unit % 2 * (width // 2) + unit // 2] = 1.0
    return table


def power(exponents):
    return (1 << (16 - exponents)).astype(jnp.float32) * (1.0 / 65536.0)


SHORT = pl.CostEstimate(flops=1000, bytes_accessed=1000, transcendentals=0)


def butterfly(rows, start):
    stride = start
    while stride < len(rows):
        for b in range(len(rows)):
            if b & stride == 0:
                low, high = rows[b], rows[b + stride]
                rows[b], rows[b + stride] = low + high, low - high
        stride *= 2


def in_weights_kernel(first_steps, words_ref, scales_ref, table_ref, out_ref, sums_ref):
    half = BLOCK // 2
    words_group = GROUP // 2
    groups_block = BLOCK // GROUP
    step = pl.program_id(0)
    width = words_ref.shape[3]
    block_count = out_ref.shape[0]

    @pl.when(step < first_steps)
    def _():
        sums = []
        for q in range(FIRST):
            words = words_ref[0, 0, q * half : (q + 1) * half, :]
            pieces = []
            for shift in (0, 4):
                codes = ((words >> shift) & 15).astype(jnp.float32) - 8.0
                for g in range(groups_block):
                    at = q * groups_block + g
                    factor = power(scales_ref[0, 0, at : at + 1, :])
                    pieces.append(codes[g * words_group : (g + 1) * words_group] * factor)
            block = jnp.concatenate(pieces, axis=0).astype(jnp.bfloat16)
            sums.append(jnp.dot(table_ref[...], block, preferred_element_type=jnp.float32))
        butterfly(sums, 1)
        for q in range(FIRST):
            sums_ref[step * FIRST + q] = sums[q]

    @pl.when(step >= first_steps)
    def _():
        base = (step - first_steps) * SECOND
        for r in range(0, SECOND, 16):
            for c in range(0, width, 128):
                for q in range(FIRST):
                    rows = [
                        sums_ref[b * FIRST + q, pl.ds(pl.multiple_of(base + r, 16), 16), c : c + 128]
                        for b in range(block_count // FIRST)
                    ]
                    butterfly(rows, 1)
                    for b, row in enumerate(rows):
                        out_ref[b * FIRST + q, r : r + 16, c : c + 128] = row.astype(jnp.bfloat16)


def in_weights(words, scales, table, layer_idx):
    _, _, word_rows, width = words.shape
    full = 2 * word_rows
    block_count = full // BLOCK
    first_steps = block_count // FIRST
    word_tile = FIRST * BLOCK // 2
    group_tile = FIRST * BLOCK // GROUP
    out = pl.pallas_call(
        functools.partial(in_weights_kernel, first_steps),
        grid=(first_steps + BLOCK // SECOND,),
        in_specs=[
            pl.BlockSpec(
                (1, 1, word_tile, width),
                lambda i: (layer_idx, 0, jnp.minimum(i, first_steps - 1), 0),
            ),
            pl.BlockSpec(
                (1, 1, group_tile, width),
                lambda i: (layer_idx, 0, jnp.minimum(i, first_steps - 1), 0),
            ),
            pl.BlockSpec((BLOCK, BLOCK), lambda i: (0, 0)),
        ],
        out_specs=pl.BlockSpec(
            (block_count, SECOND, width), lambda i: (0, jnp.maximum(i - first_steps, 0), 0)
        ),
        out_shape=jax.ShapeDtypeStruct((block_count, BLOCK, width), jnp.bfloat16),
        scratch_shapes=[pltpu.VMEM((block_count, BLOCK, width), jnp.float32)],
        compiler_params=pltpu.CompilerParams(vmem_limit_bytes=54 * MIB),
        cost_estimate=SHORT,
        name="in_weights",
    )(words, scales, table)
    return out.reshape(full, width)


def out_weights_kernel(words_ref, scales_ref, out_ref):
    words = words_ref[0, 0]
    word_rows = words.shape[0]
    words_group = GROUP // 2
    for part, shift in enumerate((0, 4)):
        codes = ((words >> shift) & 15).astype(jnp.float32) - 8.0
        for g in range(word_rows // words_group):
            factor = power(scales_ref[0, 0, pl.ds(g, 1), :])
            out_ref[pl.ds(part * word_rows + g * words_group, words_group), :] = (
                codes[g * words_group : (g + 1) * words_group] * factor
            ).astype(jnp.bfloat16)


def out_weights(words, scales, layer_idx):
    _, _, word_rows, width = words.shape
    groups = scales.shape[2]
    tile = 1024
    return pl.pallas_call(
        out_weights_kernel,
        grid=(width // tile,),
        in_specs=[
            pl.BlockSpec((1, 1, word_rows, tile), lambda c: (layer_idx, 0, 0, c)),
            pl.BlockSpec((1, 1, groups, tile), lambda c: (layer_idx, 0, 0, c)),
        ],
        out_specs=pl.BlockSpec((2 * word_rows, tile), lambda c: (0, c)),
        out_shape=jax.ShapeDtypeStruct((2 * word_rows, width), jnp.bfloat16),
        compiler_params=pltpu.CompilerParams(vmem_limit_bytes=54 * MIB),
        cost_estimate=SHORT,
        name="out_weights",
    )(words, scales)


def expert_kernel(part_count, full_width, index_ref, *refs):
    x_refs = refs[:part_count]
    gain_ref, gate_ref, up_ref, down_ref, split_ref = refs[part_count : part_count + 5]
    out_refs = refs[part_count + 5 : 2 * part_count + 5]
    gate_acc, up_acc, square_acc, act_ref = refs[2 * part_count + 5 :]
    step = pl.program_id(0)

    for j in range(part_count):

        @pl.when(step == j)
        def _(j=j):
            rows = x_refs[j][...]
            wide = rows.astype(jnp.float32)
            rows = (wide * gain_ref[...]).astype(jnp.bfloat16)
            gate = jnp.dot(rows, gate_ref[...], preferred_element_type=jnp.float32)
            up = jnp.dot(rows, up_ref[...], preferred_element_type=jnp.float32)
            square = jnp.sum(wide * wide, axis=1, keepdims=True)
            if j > 0:
                gate = gate + gate_acc[...]
                up = up + up_acc[...]
                square = square + square_acc[...]
            if j < part_count - 1:
                gate_acc[...] = gate
                up_acc[...] = up
                square_acc[...] = square
            else:
                scale = lax.rsqrt(square / full_width + 1e-05) * (1.0 / math.sqrt(full_width))
                gate = gate * scale
                act = (gate / (1.0 + jnp.exp(-gate))) * (up * scale)
                act_ref[...] = jnp.dot(
                    act.astype(jnp.bfloat16), split_ref[...], preferred_element_type=jnp.float32
                ).astype(jnp.bfloat16)

    for j in range(part_count):

        @pl.when(step == part_count + j)
        def _(j=j):
            out_refs[j][...] = jnp.dot(
                act_ref[...], down_ref[...], preferred_element_type=jnp.float32
            ).astype(jnp.bfloat16)


def expert_parts(index, parts, gain, gate_w, up_w, down_w, split):
    part_count = len(parts)
    row_count, width = parts[0].shape
    full_width, hidden = gate_w.shape
    whole = pl.BlockSpec((row_count, width), lambda i, t: (0, 0))
    last = part_count - 1
    in_block = pl.BlockSpec((width, hidden), lambda i, t: (jnp.minimum(i, last) ^ t[0], 0))
    return pl.pallas_call(
        functools.partial(expert_kernel, part_count, full_width),
        grid_spec=pltpu.PrefetchScalarGridSpec(
            num_scalar_prefetch=1,
            grid=(2 * part_count,),
            in_specs=[whole] * part_count
            + [
                pl.BlockSpec((1, width), lambda i, t: (0, jnp.minimum(i, last) ^ t[0])),
                in_block,
                in_block,
                pl.BlockSpec(
                    (hidden, width), lambda i, t: (0, jnp.maximum(i - part_count, 0) ^ t[0])
                ),
                pl.BlockSpec((hidden, hidden), lambda i, t: (0, 0)),
            ],
            out_specs=[whole] * part_count,
            scratch_shapes=[
                pltpu.VMEM((row_count, hidden), jnp.float32),
                pltpu.VMEM((row_count, hidden), jnp.float32),
                pltpu.VMEM((row_count, 1), jnp.float32),
                pltpu.VMEM((row_count, hidden), jnp.bfloat16),
            ],
        ),
        out_shape=[jax.ShapeDtypeStruct((row_count, width), jnp.bfloat16)] * part_count,
        compiler_params=pltpu.CompilerParams(vmem_limit_bytes=40 * MIB),
        cost_estimate=SHORT,
        name="expert_parts",
    )(index, *parts, gain, gate_w, up_w, down_w, split)


def add_split_kernel(term_count, *refs):
    total = refs[0][...].astype(jnp.float32)
    for term in refs[1:term_count]:
        total = total + term[...].astype(jnp.float32)
    at = 0
    for out in refs[term_count:]:
        rows = out.shape[0]
        out[...] = total[at : at + rows].astype(jnp.bfloat16)
        at += rows


def add_split(terms, piece_rows):
    row_count, width = terms[0].shape
    return pl.pallas_call(
        functools.partial(add_split_kernel, len(terms)),
        out_shape=[
            jax.ShapeDtypeStruct((piece_rows, width), jnp.bfloat16)
            for _ in range(row_count // piece_rows)
        ],
        compiler_params=pltpu.CompilerParams(vmem_limit_bytes=32 * MIB),
        cost_estimate=SHORT,
        name="add_split",
    )(*terms)


def make_stats(stream, gain, router):
    scaled = (stream * gain).astype(jnp.bfloat16)
    logits = lax.dot_general(router, scaled, NT, preferred_element_type=jnp.float32)
    squares = stream * stream
    high = squares.astype(jnp.bfloat16)
    low = (squares - high.astype(jnp.float32)).astype(jnp.bfloat16)
    ones = jnp.ones((8, stream.shape[1]), jnp.bfloat16)
    square = lax.dot_general(ones, high, NT, preferred_element_type=jnp.float32) + lax.dot_general(
        ones, low, NT, preferred_element_type=jnp.float32
    )
    return logits, square


def fill_slots(picks, rows, slot_refs):
    gathered = jnp.dot(picks, rows, preferred_element_type=jnp.float32)
    capacity = slot_refs[0].shape[0]
    for k, out in enumerate(slot_refs):
        out[...] = gathered[k * capacity : (k + 1) * capacity].astype(jnp.bfloat16)


def enter_kernel(expert_count, me_ref, routes_ref, tokens_ref, gain_ref, router_ref, *refs):
    picks_ref, stats_ref = refs[:2]
    slot_refs = refs[2:]
    token_count = tokens_ref.shape[0]
    capacity = slot_refs[0].shape[0]
    relative = lax.broadcasted_iota(jnp.int32, (expert_count, token_count), 0) ^ me_ref[0]
    first, second = routes_ref[0:1, :], routes_ref[1:2, :]
    member = ((relative == first) | (relative == second)).astype(jnp.float32)
    before = lax.broadcasted_iota(jnp.int32, (token_count, token_count), 0)
    after = lax.broadcasted_iota(jnp.int32, (token_count, token_count), 1)
    earlier = (before < after).astype(jnp.bfloat16)
    ranks = jnp.dot(member.astype(jnp.bfloat16), earlier, preferred_element_type=jnp.float32)
    position = lax.broadcasted_iota(jnp.int32, (capacity, token_count), 0).astype(jnp.float32)
    pieces = [
        jnp.where(position == ranks[k : k + 1, :], member[k : k + 1, :], 0.0)
        for k in range(expert_count)
    ]
    picks = jnp.concatenate(pieces, axis=0).astype(jnp.bfloat16)
    picks_ref[...] = picks
    tokens = tokens_ref[...]
    fill_slots(picks, tokens, slot_refs)
    logits, square = make_stats(tokens.astype(jnp.float32), gain_ref[...], router_ref[...])
    stats_ref[0:expert_count, :] = logits
    stats_ref[expert_count:, :] = square


def enter(me, routes, tokens, gain, router, capacity):
    token_count, width = tokens.shape
    expert_count = router.shape[0]
    vmem = pl.BlockSpec(memory_space=pltpu.VMEM)
    return pl.pallas_call(
        functools.partial(enter_kernel, expert_count),
        in_specs=[pl.BlockSpec(memory_space=pltpu.SMEM)] + [vmem] * 4,
        out_shape=[
            jax.ShapeDtypeStruct((expert_count * capacity, token_count), jnp.bfloat16),
            jax.ShapeDtypeStruct((expert_count + 8, token_count), jnp.float32),
        ]
        + [jax.ShapeDtypeStruct((capacity, width), jnp.bfloat16)] * expert_count,
        compiler_params=pltpu.CompilerParams(vmem_limit_bytes=32 * MIB),
        cost_estimate=SHORT,
        name="enter",
    )(me, routes, tokens, gain, router)


def combine_kernel(expert_count, piece_count, full_width, last, me_ref, *refs):
    routes_ref, picks_ref, stats_ref, stream_ref = refs[:4]
    piece_refs = refs[4 : 4 + piece_count]
    rest = refs[4 + piece_count :]
    token_count = stream_ref.shape[0]
    capacity = picks_ref.shape[0] // expert_count
    first, second = routes_ref[0:1, :], routes_ref[1:2, :]
    logits = stats_ref[0:expert_count, :]
    scale = lax.rsqrt(stats_ref[expert_count : expert_count + 1, :] / full_width + 1e-05)
    expert = lax.broadcasted_iota(jnp.int32, (expert_count, token_count), 0)
    first_logit = jnp.sum(jnp.where(expert == first, logits, 0.0), axis=0, keepdims=True)
    second_logit = jnp.sum(jnp.where(expert == second, logits, 0.0), axis=0, keepdims=True)
    first_weight = 1.0 / (1.0 + jnp.exp((second_logit - first_logit) * scale))
    second_weight = 1.0 - first_weight
    relative = expert ^ me_ref[0]
    weight = jnp.where(relative == first, first_weight, 0.0) + jnp.where(
        relative == second, second_weight, 0.0
    )
    picks = picks_ref[...]
    wide_picks = picks.astype(jnp.float32)
    weighted = jnp.concatenate(
        [
            wide_picks[k * capacity : (k + 1) * capacity] * weight[k : k + 1, :]
            for k in range(expert_count)
        ],
        axis=0,
    )
    high = weighted.astype(jnp.bfloat16)
    low = (weighted - high.astype(jnp.float32)).astype(jnp.bfloat16)
    outs = [piece[...] for piece in piece_refs]
    outs = outs[0] if len(outs) == 1 else jnp.concatenate(outs, axis=0)
    added = lax.dot_general(high, outs, TN, preferred_element_type=jnp.float32)
    added = added + lax.dot_general(low, outs, TN, preferred_element_type=jnp.float32)
    stream = stream_ref[...].astype(jnp.float32) + added
    if last:
        rest[0][...] = stream.astype(jnp.bfloat16)
        return
    gain_ref, router_ref, next_ref, next_stats_ref = rest[:4]
    next_ref[...] = stream
    fill_slots(picks, stream.astype(jnp.bfloat16), rest[4:])
    logits, square = make_stats(stream, gain_ref[...], router_ref[...])
    next_stats_ref[0:expert_count, :] = logits
    next_stats_ref[expert_count:, :] = square


def combine(me, routes, picks, stats, stream, pieces, full_width, following):
    token_count, width = stream.shape
    expert_count = stats.shape[0] - 8
    capacity = picks.shape[0] // expert_count
    if capacity % 16:
        pieces = [jnp.concatenate(pieces, axis=0)]
    vmem = pl.BlockSpec(memory_space=pltpu.VMEM)
    operands = [routes, picks, stats, stream, *pieces]
    if following is None:
        out_shape = [jax.ShapeDtypeStruct((token_count, width), jnp.bfloat16)]
    else:
        operands += following
        out_shape = [
            jax.ShapeDtypeStruct((token_count, width), jnp.float32),
            jax.ShapeDtypeStruct(stats.shape, jnp.float32),
        ] + [jax.ShapeDtypeStruct((capacity, width), jnp.bfloat16)] * expert_count
    return pl.pallas_call(
        functools.partial(
            combine_kernel, expert_count, len(pieces), full_width, following is None
        ),
        in_specs=[pl.BlockSpec(memory_space=pltpu.SMEM)] + [vmem] * len(operands),
        out_shape=out_shape,
        compiler_params=pltpu.CompilerParams(vmem_limit_bytes=32 * MIB),
        cost_estimate=SHORT,
        name="combine",
    )(me, *operands)


def ordered(value, *earlier):
    return lax.optimization_barrier((value, earlier))[0]


def gather_parts(parts, bits):
    parts = dict(parts)
    for bit in bits:
        for j in sorted(parts):
            parts[j ^ 1 << bit] = exchange(parts[j], "tensor", 1 << bit)
    return parts


def reduce_parts(terms, bit):
    kept = {j: list(parts) for j, parts in terms.items() if not j >> bit & 1}
    for j, parts in terms.items():
        if j >> bit & 1:
            total = parts[0]
            if len(parts) > 1:
                total = sum(part.astype(jnp.float32) for part in parts).astype(jnp.bfloat16)
            kept[j ^ 1 << bit].append(exchange(total, "tensor", 1 << bit))
    return kept


def settle(terms):
    return {
        j: parts
        if j == 0 or len(parts) == 1
        else [sum(part.astype(jnp.float32) for part in parts).astype(jnp.bfloat16)]
        for j, parts in terms.items()
    }


def per_device(
    tokens,
    routes,
    norm_gain,
    router_weight,
    gate_codes,
    gate_scales,
    up_codes,
    up_scales,
    down_codes,
    down_scales,
):
    part_count = lax.axis_size("tensor")
    expert_count = lax.axis_size("expert")
    bits = part_count.bit_length() - 1
    token_count, width = tokens.shape
    full_width = width * part_count
    hidden = gate_codes.shape[3]
    capacity = 3 * token_count // expert_count
    me = lax.axis_index("expert").astype(jnp.int32).reshape(1)
    index = lax.axis_index("tensor").astype(jnp.int32).reshape(1)
    table = jnp.asarray(block_table(), jnp.bfloat16)
    split = jnp.asarray(split_table(hidden), jnp.bfloat16)
    routes_rows = routes.T
    router_rows = jnp.swapaxes(router_weight, 1, 2)

    picks, stats, *slots = enter(
        me, routes_rows, tokens, norm_gain[0:1], router_rows[0], capacity
    )
    whole_gain = lax.all_gather(norm_gain, "tensor", axis=1, tiled=True)

    quarter = expert_count // 4
    near = list(range(2 * quarter))
    far = [list(range(2 * quarter, 3 * quarter)), list(range(3 * quarter, 4 * quarter))]
    first_bits, core_bits = list(reversed(range(1, bits))), [0]
    stream = tokens

    def stack(pieces, *earlier):
        return jnp.concatenate(ordered(pieces, *earlier), axis=0)

    def gather_first(rows):
        return gather_parts({0: rows}, first_bits)

    def cores_added(outs):
        return settle(reduce_parts({j: [part] for j, part in enumerate(outs)}, 0))

    def rest_added(terms):
        for bit in range(1, bits):
            terms = reduce_parts(terms, bit)
        return terms[0]

    def give_back(terms, chunk, returned):
        pieces = add_split(terms, capacity)
        for k, piece in zip(chunk, pieces):
            returned[k] = piece if k == 0 else exchange(piece, "expert", k)
        return pieces

    weights = None
    for layer_idx in range(LAYERS):
        gain = whole_gain[layer_idx : layer_idx + 1]
        arrived = [slots[0]] + [
            exchange(slots[k], "expert", k) for k in range(1, expert_count)
        ]
        returned = [None] * expert_count
        near_parts = gather_first(stack([arrived[k] for k in near]))
        if weights is None:
            later = ordered(table, near_parts[0])
            gate_w = in_weights(gate_codes, gate_scales, later, layer_idx)
            near_parts = ordered(near_parts, gate_w)
            later = ordered(table, near_parts)
            near_parts = gather_parts(near_parts, core_bits)
            up_w = in_weights(up_codes, up_scales, later, layer_idx)
            down_w = out_weights(down_codes, ordered(down_scales, up_w), layer_idx)
            weights = (gate_w, up_w, down_w)
            far_rows = stack([arrived[k] for k in far[0]], up_w)
        else:
            near_parts = gather_parts(near_parts, core_bits)
            far_rows = stack([arrived[k] for k in far[0]])
        for bit in range(bits):
            stats = stats + exchange(stats, "tensor", 1 << bit)
        one_parts = gather_first(far_rows)

        def experts(parts, *earlier):
            turn = ordered(index, *earlier)
            return expert_parts(
                turn, [parts[j] for j in range(part_count)], gain, *weights, split
            )

        near_outs = experts(near_parts, far_rows)
        one_parts = gather_parts(ordered(one_parts, near_outs), core_bits)
        far_rows = stack([arrived[k] for k in far[1]], near_outs)
        one_outs = experts(one_parts, near_outs, far_rows)
        two_parts = gather_parts(gather_first(far_rows), core_bits)
        one_terms = cores_added(one_outs)
        one_pieces = give_back(rest_added(one_terms), far[0], returned)
        two_outs = experts(two_parts, one_pieces)
        two_terms = cores_added(two_outs)
        near_terms = cores_added(ordered(near_outs, one_outs))
        near_terms = rest_added(ordered(near_terms, two_terms))
        two_terms = rest_added(two_terms)
        following = None
        if layer_idx + 1 < LAYERS:
            following = [norm_gain[layer_idx + 1 : layer_idx + 2], router_rows[layer_idx + 1]]
            later = ordered(table, two_outs)
            gate_w = in_weights(gate_codes, gate_scales, later, layer_idx + 1)
            two_terms = ordered(two_terms, gate_w)
            two_pieces = give_back(two_terms, far[1], returned)
            later = ordered(table, two_pieces)
            up_w = in_weights(up_codes, up_scales, later, layer_idx + 1)
            near_terms = ordered(near_terms, up_w)
            give_back(near_terms, near, returned)
            down_w = out_weights(down_codes, ordered(down_scales, near_terms), layer_idx + 1)
            weights = (gate_w, up_w, down_w)
            me = ordered(me, weights)
        else:
            two_pieces = give_back(two_terms, far[1], returned)
            give_back(ordered(near_terms, two_pieces), near, returned)
        results = combine(
            me, routes_rows, picks, stats, stream, returned, full_width, following
        )
        if following is None:
            return results[0]
        stream, stats, *slots = results


def solution(mesh):
    in_specs = (
        P("expert", "tensor"),
        P("expert", None),
        P(None, "tensor"),
        P(None, "tensor", None),
        P(None, "expert", None, "tensor"),
        P(None, "expert", None, "tensor"),
        P(None, "expert", None, "tensor"),
        P(None, "expert", None, "tensor"),
        P(None, "expert", "tensor", None),
        P(None, "expert", "tensor", None),
    )
    out_specs = P("expert", "tensor")
    return jax.shard_map(
        per_device, mesh=mesh, in_specs=in_specs, out_specs=out_specs, check_vma=False
    )
```

time: 722 us -> 316 us (0.44); the launches traced: 711 us -> 314 us
  blocking collectives: 171 us -> 10.3 us
  local copies, waits for them, and re-layouts: 165 us -> 6.72 us
  waiting for transfers between devices: 251 us -> 118 us
  Pallas kernels: 0 us -> 108 us
  starting transfers between devices: 17.7 us -> 69.8 us
  other arithmetic: 49.8 us -> 0.94 us
  matrix products: 42.6 us -> 0 us
  between operations: 13.7 us -> 0.53 us
    all_to_all x1 -> x0, blocking collectives: 144 us -> none  [per_device(): lax.all_to_all(outgoing, 'expert', split_axis=0, concat_axis=0, tiled=True)]
    shift_right_arithmetic x18 -> x0, local copies, waits for them, and re-layouts: 118 us -> none  [unpack(): jnp.right_shift(words[:, None, :], shifts[None, :, None])]
    reduce_scatter x2 -> x0, waiting for transfers between devices: 116 us -> none  [per_device(): lax.psum_scatter(partial_value.astype(jnp.bfloat16), 'tensor', scatter_di...]
    pallas_call x0 -> x21, Pallas kernels: none -> 108 us  [the longest x6 43.6 us: expert_parts(): pl.pallas_call(functools.partial(expert_kernel, part_count, full_width),...]
    ppermute x4 -> x68, waiting for transfers between devices: 31.1 us -> 118 us  [exchange(): lax.ppermute(shard, axis, [(i, i ^ mask) for i in range(lax.axis_size(axi...]
    ppermute x4 -> x68, starting transfers between devices: 0.9 us -> 69.8 us  [exchange(): lax.ppermute(shard, axis, [(i, i ^ mask) for i in range(lax.axis_size(axi...]
    all_to_all x3 -> x0, waiting for transfers between devices: 60.8 us -> none  [the longest x2 60.8 us: per_device(): lax.all_to_all(reduced, 'expert', split_axis=0, concat_axis=0, tiled=True)]
    all_gather x2 -> x0, waiting for transfers between devices: 43.1 us -> none  [per_device(): whole = lax.all_gather(moving, 'tensor', axis=1, tiled=True)]
  transfers between devices with their start and end apart: 11 -> 68, of which waited for: 10 -> 31; matrix products, arithmetic and copies ran while one was open for 21% -> 1% of each run, Pallas kernels for 0% -> 29%
where the time goes in v1:
time: 316 us; the launch traced here: 314 us
  waiting for transfers between devices  118 us (37%)
  Pallas kernels  108 us (34%)
  starting transfers between devices  69.8 us (22%)
  blocking collectives  10.3 us (3%)
  local copies, waits for them, and re-layouts  6.72 us (2%)
    ppermute x68, waiting for transfers between devices, exchange(): lax.ppermute(shard, axis, [(i, i ^ mask) for i in range(lax.axis_size(axi...  118 us
    ppermute x68, starting transfers between devices, exchange(): lax.ppermute(shard, axis, [(i, i ^ mask) for i in range(lax.axis_size(axi...  69.8 us
    pallas_call x6, Pallas kernels, expert_parts(): pl.pallas_call(functools.partial(expert_kernel, part_count, full_width),...  43.6 us
    pallas_call x4, Pallas kernels, in_weights(): pl.pallas_call(functools.partial(in_weights_kernel, first_steps), grid=(f...  43 us
    pallas_call x2, Pallas kernels, out_weights(): pl.pallas_call(out_weights_kernel, grid=(width // tile,), in_specs=[pl.Bl...  15.1 us
    all_gather x1, blocking collectives, per_device(): whole_gain = lax.all_gather(norm_gain, 'tensor', axis=1, tiled=True)  10.3 us
  transfers between devices with their start and end apart: 68, of which 31 were waited for; matrix products, arithmetic and copies ran while one was open for 1% of the time, Pallas kernels for 29%

profile of v1, /device:TPU:0, one launch (start us, length us, event | category | flops | bytes accessed | tf_op | source)
XLA Modules:
  0.0 314.0 jit_solution(1306525416813436244)
XLA Ops:
  3.9 1.6 enter.1
  5.5 3.0 collective-permute-start.2
  8.5 1.6 collective-permute-start.3
  10.0 3.3 %collective-permute-done.2 = bf16[48,2048]{1,0:T(8,128)(2,1)S(1)} collective-permute-done((bf16[48,2048]{1,0:T(8,128)(2,1)S(1)}, bf16[48,2048]{1,0:T(8,128)(2,1)S(1)}, u32[]{:S(2)}, u32[]{:S(2)}) %collective-permute-start.2) | collective-permute-done | bytes 196640 | tf_op jit(solution)/shard_map/ppermute | solution.py:23
  13.4 2.9 collective-permute-done.3
  16.3 2.5 collective-permute-done.4
  18.9 1.7 collective-permute-start.5
  20.6 2.6 collective-permute-start
  24.5 3.6 %collective-permute-start.8 = (bf16[48,2048]{1,0:T(8,128)(2,1)}, bf16[48,2048]{1,0:T(8,128)(2,1)}, u32[]{:S(2)}, u32[]{:S(2)}) collective-permute-start(bf16[48,2048]{1,0:T(8,128)(2,1)} %get-tuple-element.145), channel_id=1, source_target_pairs={{0,24},{4,28},{8,16},{12,20},{16,8},{20,12},{24,0},{28,4},{1,25},{... | collective-permute-start | bytes 589832 | tf_op jit(solution)/shard_map/ppermute | solution.py:23
  28.3 10.3 %all_gather.3 = f32[2,8192]{1,0:T(2,128)S(1)} all-gather(f32[2,2048]{1,0:T(2,128)} %param.14), channel_id=1, replica_groups=mesh['expert'=8,'tensor'=4] {'tensor'}, dimensions={1}, use_global_device_ids=true | all-gather | bytes 81920 | tf_op jit(solution)/shard_map/all_gather | solution.py:466
  38.6 10.7 %in_weights.4 = bf16[32,256,256]{2,1,0:T(8,128)(2,1)} custom-call(s32[2,1,4096,256]{3,2,1,0:T(8,128)} %words_ref.9, s32[2,1,64,256]{3,2,1,0:T(8,128)} %scales_ref.7, bf16[256,256]{1,0:T(8,128)(2,1)} %constant.13.clone.table_ref), custom_call_target="tpu_custom_call" | custom-call | flops 1000 | bytes 1000 | tf_op jit(solution)/shard_map/in_weights/pallas_call | solution.py:106
  49.6 10.8 %in_weights.5 = bf16[32,256,256]{2,1,0:T(8,128)(2,1)} custom-call(s32[2,1,4096,256]{3,2,1,0:T(8,128)} %words_ref.10, s32[2,1,64,256]{3,2,1,0:T(8,128)} %scales_ref.8, bf16[256,256]{1,0:T(8,128)(2,1)} %constant.13.clone.table_ref), custom_call_target="tpu_custom_call" | custom-call | flops 1000 | bytes 1000 | tf_op jit(solution)/shard_map/in_weights/pallas_call | solution.py:106
  62.7 7.8 %out_weights.2.refs_7_ = bf16[256,8192]{1,0:T(8,128)(2,1)} custom-call(s32[2,1,128,8192]{3,2,1,0:T(8,128)} %words_ref.11, s32[2,1,2,8192]{3,2,1,0:T(2,128)} %scales_ref.9), custom_call_target="tpu_custom_call" | custom-call | flops 1000 | bytes 1000 | tf_op jit(solution)/shard_map/out_weights/pallas_call | solution.py:149
  70.5 8.4 %expert_parts.6 = (bf16[192,2048]{1,0:T(8,128)(2,1)S(1)}, bf16[192,2048]{1,0:T(8,128)(2,1)S(1)}, bf16[192,2048]{1,0:T(8,128)(2,1)S(1)}, bf16[192,2048]{1,0:T(8,128)(2,1)S(1)}) custom-call(s32[1]{0:T(128)} %bitcast.1.index_ref, bf16[192,2048]{1,0:T(8,128)(2,1)S(1)} %constant_dynamic-update-slice_fusion.refs_0_, ...), custom_call_target="tpu_custom_call" | custom-call | flops 1000 | bytes 1000 | tf_op jit(solution)/shard_map/expert_parts/pallas_call | solution.py:213
  81.5 6.7 %expert_parts.7 = (bf16[96,2048]{1,0:T(8,128)(2,1)S(1)}, bf16[96,2048]{1,0:T(8,128)(2,1)S(1)}, bf16[96,2048]{1,0:T(8,128)(2,1)S(1)}, bf16[96,2048]{1,0:T(8,128)(2,1)S(1)}) custom-call(s32[1]{0:T(128)} %bitcast.1.index_ref, bf16[96,2048]{1,0:T(8,128)(2,1)S(1)} %constant_dynamic-update-slice_fusion.4.refs_0_, ...), custom_call_target="tpu_custom_call" | custom-call | flops 1000 | bytes 1000 | tf_op jit(solution)/shard_map/expert_parts/pallas_call | solution.py:213
  91.1 9.2 %collective-permute-done.17.refs_2_ = bf16[96,2048]{1,0:T(8,128)(2,1)S(1)} collective-permute-done((bf16[96,2048]{1,0:T(8,128)(2,1)S(1)}, bf16[96,2048]{1,0:T(8,128)(2,1)S(1)}, u32[]{:S(2)}, u32[]{:S(2)}) %collective-permute-start.17) | collective-permute-done | bytes 393248 | tf_op jit(solution)/shard_map/ppermute | solution.py:23
  100.9 7.4 %collective-permute-done.15.refs_2_ = bf16[96,2048]{1,0:T(8,128)(2,1)S(1)} collective-permute-done((bf16[96,2048]{1,0:T(8,128)(2,1)S(1)}, bf16[96,2048]{1,0:T(8,128)(2,1)S(1)}, u32[]{:S(2)}, u32[]{:S(2)}) %collective-permute-start.15) | collective-permute-done | bytes 393248 | tf_op jit(solution)/shard_map/ppermute | solution.py:23
  108.4 6.6 %expert_parts.8 = (bf16[96,2048]{1,0:T(8,128)(2,1)S(1)}, bf16[96,2048]{1,0:T(8,128)(2,1)S(1)}, bf16[96,2048]{1,0:T(8,128)(2,1)S(1)}, bf16[96,2048]{1,0:T(8,128)(2,1)S(1)}) custom-call(s32[1]{0:T(128)} %bitcast.1.index_ref, bf16[96,2048]{1,0:T(8,128)(2,1)S(1)} %constant_dynamic-update-slice_fusion.6.refs_0_, ...), custom_call_target="tpu_custom_call" | custom-call | flops 1000 | bytes 1000 | tf_op jit(solution)/shard_map/expert_parts/pallas_call | solution.py:213
  119.6 2.6 collective-permute-start.30
  125.2 10.7 %in_weights.6 = bf16[32,256,256]{2,1,0:T(8,128)(2,1)} custom-call(s32[2,1,4096,256]{3,2,1,0:T(8,128)} %words_ref.9, s32[2,1,64,256]{3,2,1,0:T(8,128)} %scales_ref.7, bf16[256,256]{1,0:T(8,128)(2,1)} %constant.13.clone.table_ref), custom_call_target="tpu_custom_call" | custom-call | flops 1000 | bytes 1000 | tf_op jit(solution)/shard_map/in_weights/pallas_call | solution.py:106
  135.9 9.7 %collective-permute-done.21.refs_2_ = bf16[96,2048]{1,0:T(8,128)(2,1)S(1)} collective-permute-done((bf16[96,2048]{1,0:T(8,128)(2,1)S(1)}, bf16[96,2048]{1,0:T(8,128)(2,1)S(1)}, u32[]{:S(2)}, u32[]{:S(2)}) %collective-permute-start.21) | collective-permute-done | bytes 393248 | tf_op jit(solution)/shard_map/ppermute | solution.py:23
  145.8 3.7 %collective-permute-start.32 = (bf16[48,2048]{1,0:T(8,128)(2,1)S(1)}, bf16[48,2048]{1,0:T(8,128)(2,1)S(1)}, u32[]{:S(2)}, u32[]{:S(2)}) collective-permute-start(bf16[48,2048]{1,0:T(8,128)(2,1)S(1)} %get-tuple-element.167), channel_id=1, source_target_pairs={{0,24},{4,28},{8,16},{12,20},{16,8},{20,12},{24,0},{28,4},{1,25},{... | collective-permute-start | bytes 589832 | tf_op jit(solution)/shard_map/ppermute | solution.py:23
  149.5 10.7 %in_weights.7 = bf16[32,256,256]{2,1,0:T(8,128)(2,1)} custom-call(s32[2,1,4096,256]{3,2,1,0:T(8,128)} %words_ref.10, s32[2,1,64,256]{3,2,1,0:T(8,128)} %scales_ref.8, bf16[256,256]{1,0:T(8,128)(2,1)} %constant.13.clone.table_ref), custom_call_target="tpu_custom_call" | custom-call | flops 1000 | bytes 1000 | tf_op jit(solution)/shard_map/in_weights/pallas_call | solution.py:106
  162.3 3.0 collective-permute-start.29
  165.3 7.3 %out_weights.3.refs_7_ = bf16[256,8192]{1,0:T(8,128)(2,1)} custom-call(s32[2,1,128,8192]{3,2,1,0:T(8,128)} %words_ref.11, s32[2,1,2,8192]{3,2,1,0:T(2,128)} %scales_ref.9), custom_call_target="tpu_custom_call" | custom-call | flops 1000 | bytes 1000 | tf_op jit(solution)/shard_map/out_weights/pallas_call | solution.py:149
  173.1 3.8 %collective-permute-done.29.refs_7_ = bf16[48,2048]{1,0:T(8,128)(2,1)S(1)} collective-permute-done((bf16[48,2048]{1,0:T(8,128)(2,1)S(1)}, bf16[48,2048]{1,0:T(8,128)(2,1)S(1)}, u32[]{:S(2)}, u32[]{:S(2)}) %collective-permute-start.29) | collective-permute-done | bytes 196640 | tf_op jit(solution)/shard_map/ppermute | solution.py:23
  176.9 1.6 combine.2
  179.1 2.9 collective-permute-start.40
  182.0 3.4 %collective-permute-done.38 = bf16[48,2048]{1,0:T(8,128)(2,1)S(1)} collective-permute-done((bf16[48,2048]{1,0:T(8,128)(2,1)S(1)}, bf16[48,2048]{1,0:T(8,128)(2,1)S(1)}, u32[]{:S(2)}, u32[]{:S(2)}) %collective-permute-start.38) | collective-permute-done | bytes 196640 | tf_op jit(solution)/shard_map/ppermute | solution.py:23
  186.9 3.6 %collective-permute-done.40 = bf16[48,2048]{1,0:T(8,128)(2,1)S(1)} collective-permute-done((bf16[48,2048]{1,0:T(8,128)(2,1)S(1)}, bf16[48,2048]{1,0:T(8,128)(2,1)S(1)}, u32[]{:S(2)}, u32[]{:S(2)}) %collective-permute-start.40) | collective-permute-done | bytes 196640 | tf_op jit(solution)/shard_map/ppermute | solution.py:23
  191.3 2.7 collective-permute-start.37
  193.9 11.9 %collective-permute-done.36 = bf16[48,2048]{1,0:T(8,128)(2,1)S(1)} collective-permute-done((bf16[48,2048]{1,0:T(8,128)(2,1)S(1)}, bf16[48,2048]{1,0:T(8,128)(2,1)S(1)}, u32[]{:S(2)}, u32[]{:S(2)}) %collective-permute-start.36) | collective-permute-done | bytes 196640 | tf_op jit(solution)/shard_map/ppermute | solution.py:23
  205.9 3.6 %collective-permute-done.37 = bf16[48,2048]{1,0:T(8,128)(2,1)S(1)} collective-permute-done((bf16[48,2048]{1,0:T(8,128)(2,1)S(1)}, bf16[48,2048]{1,0:T(8,128)(2,1)S(1)}, u32[]{:S(2)}, u32[]{:S(2)}) %collective-permute-start.37) | collective-permute-done | bytes 196640 | tf_op jit(solution)/shard_map/ppermute | solution.py:23
  211.3 4.9 %collective-permute-start.45 = (bf16[48,2048]{1,0:T(8,128)(2,1)S(1)}, bf16[48,2048]{1,0:T(8,128)(2,1)S(1)}, u32[]{:S(2)}, u32[]{:S(2)}) collective-permute-start(bf16[48,2048]{1,0:T(8,128)(2,1)S(1)} %get-tuple-element.208), channel_id=1, source_target_pairs={{0,28},{4,24},{8,20},{12,16},{16,12},{20,8},{24,4},{28,0},{1,29},{... | collective-permute-start | bytes 589832 | tf_op jit(solution)/shard_map/ppermute | solution.py:23
  216.3 8.5 %expert_parts.9 = (bf16[192,2048]{1,0:T(8,128)(2,1)S(1)}, bf16[192,2048]{1,0:T(8,128)(2,1)S(1)}, bf16[192,2048]{1,0:T(8,128)(2,1)S(1)}, bf16[192,2048]{1,0:T(8,128)(2,1)S(1)}) custom-call(s32[1]{0:T(128)} %bitcast.1.index_ref, bf16[192,2048]{1,0:T(8,128)(2,1)S(1)} %constant_dynamic-update-slice_fusion.10.refs_0_, ...), custom_call_target="tpu_custom_call" | custom-call | flops 1000 | bytes 1000 | tf_op jit(solution)/shard_map/expert_parts/pallas_call | solution.py:213
  227.9 6.6 %expert_parts.10 = (bf16[96,2048]{1,0:T(8,128)(2,1)S(1)}, bf16[96,2048]{1,0:T(8,128)(2,1)S(1)}, bf16[96,2048]{1,0:T(8,128)(2,1)S(1)}, bf16[96,2048]{1,0:T(8,128)(2,1)S(1)}) custom-call(s32[1]{0:T(128)} %bitcast.1.index_ref, bf16[96,2048]{1,0:T(8,128)(2,1)S(1)} %constant_dynamic-update-slice_fusion.8.refs_0_, ...), custom_call_target="tpu_custom_call" | custom-call | flops 1000 | bytes 1000 | tf_op jit(solution)/shard_map/expert_parts/pallas_call | solution.py:213
  237.4 9.2 %collective-permute-done.55.refs_2_ = bf16[96,2048]{1,0:T(8,128)(2,1)S(1)} collective-permute-done((bf16[96,2048]{1,0:T(8,128)(2,1)S(1)}, bf16[96,2048]{1,0:T(8,128)(2,1)S(1)}, u32[]{:S(2)}, u32[]{:S(2)}) %collective-permute-start.55) | collective-permute-done | bytes 393248 | tf_op jit(solution)/shard_map/ppermute | solution.py:23
  247.1 7.4 %collective-permute-done.53.refs_2_ = bf16[96,2048]{1,0:T(8,128)(2,1)S(1)} collective-permute-done((bf16[96,2048]{1,0:T(8,128)(2,1)S(1)}, bf16[96,2048]{1,0:T(8,128)(2,1)S(1)}, u32[]{:S(2)}, u32[]{:S(2)}) %collective-permute-start.53) | collective-permute-done | bytes 393248 | tf_op jit(solution)/shard_map/ppermute | solution.py:23
  254.7 6.9 %expert_parts.11 = (bf16[96,2048]{1,0:T(8,128)(2,1)S(1)}, bf16[96,2048]{1,0:T(8,128)(2,1)S(1)}, bf16[96,2048]{1,0:T(8,128)(2,1)S(1)}, bf16[96,2048]{1,0:T(8,128)(2,1)S(1)}) custom-call(s32[1]{0:T(128)} %bitcast.1.index_ref, bf16[96,2048]{1,0:T(8,128)(2,1)S(1)} %constant_dynamic-update-slice_fusion.14.refs_0_, ...), custom_call_target="tpu_custom_call" | custom-call | flops 1000 | bytes 1000 | tf_op jit(solution)/shard_map/expert_parts/pallas_call | solution.py:213
  266.1 4.7 %collective-permute-start.64 = (bf16[48,2048]{1,0:T(8,128)(2,1)S(1)}, bf16[48,2048]{1,0:T(8,128)(2,1)S(1)}, u32[]{:S(2)}, u32[]{:S(2)}) collective-permute-start(bf16[48,2048]{1,0:T(8,128)(2,1)S(1)} %get-tuple-element.222), channel_id=1, source_target_pairs={{0,16},{4,20},{8,24},{12,28},{16,0},{20,4},{24,8},{28,12},{1,17},{... | collective-permute-start | bytes 589832 | tf_op jit(solution)/shard_map/ppermute | solution.py:23
  273.9 18.2 %collective-permute-done.60.refs_2_ = bf16[96,2048]{1,0:T(8,128)(2,1)S(1)} collective-permute-done((bf16[96,2048]{1,0:T(8,128)(2,1)S(1)}, bf16[96,2048]{1,0:T(8,128)(2,1)S(1)}, u32[]{:S(2)}, u32[]{:S(2)}) %collective-permute-start.60) | collective-permute-done | bytes 393248 | tf_op jit(solution)/shard_map/ppermute | solution.py:23
  292.7 3.0 collective-permute-start.67
  296.0 2.0 collective-permute-start.61
  298.0 1.9 collective-permute-start.62
  302.2 2.9 collective-permute-done.67.refs_11_
  306.0 2.9 collective-permute-done.62.refs_6_
  308.8 3.6 %collective-permute-done.63.refs_7_ = bf16[48,2048]{1,0:T(8,128)(2,1)S(1)} collective-permute-done((bf16[48,2048]{1,0:T(8,128)(2,1)S(1)}, bf16[48,2048]{1,0:T(8,128)(2,1)S(1)}, u32[]{:S(2)}, u32[]{:S(2)}) %collective-permute-start.63) | collective-permute-done | bytes 196640 | tf_op jit(solution)/shard_map/ppermute | solution.py:23
  312.4 1.6 combine.3
  (167 shorter events, 47.3 us)
Async XLA Ops:
  18.9 30.4 %collective-permute-start.5 = (bf16[192,2048]{1,0:T(8,128)(2,1)S(1)}, bf16[192,2048]{1,0:T(8,128)(2,1)S(1)}, u32[]{:S(2)}, u32[]{:S(2)}) collective-permute-start(bf16[192,2048]{1,0:T(8,128)(2,1)S(1)} %constant_dynamic-update-slice_fusion.refs_0_), channel_id=1, source_target_pairs={{0,2},{1,3},{2,0},{3,1},{4,6},{5,7},{6,4},{7,5},{8,10},{9,11},{10,... | collective-permute-start | bytes 2359304 | tf_op jit(solution)/shard_map/ppermute | solution.py:23
  20.6 39.8 %collective-permute-start = (bf16[48,2048]{1,0:T(8,128)(2,1)S(1)}, bf16[48,2048]{1,0:T(8,128)(2,1)S(1)}, u32[]{:S(2)}, u32[]{:S(2)}) collective-permute-start(bf16[48,2048]{1,0:T(8,128)(2,1)S(1)} %get-tuple-element.123), channel_id=1, source_target_pairs={{0,16},{4,20},{8,24},{12,28},{16,0},{20,4},{24,8},{28,12},{1,17},{... | collective-permute-start | bytes 589832 | tf_op jit(solution)/shard_map/ppermute | solution.py:23
  23.2 37.4 %collective-permute-start.1 = (bf16[48,2048]{1,0:T(8,128)(2,1)S(1)}, bf16[48,2048]{1,0:T(8,128)(2,1)S(1)}, u32[]{:S(2)}, u32[]{:S(2)}) collective-permute-start(bf16[48,2048]{1,0:T(8,128)(2,1)S(1)} %get-tuple-element.124), channel_id=1, source_target_pairs={{0,20},{4,16},{8,28},{12,24},{16,4},{20,0},{24,12},{28,8},{1,21},{... | collective-permute-start | bytes 589832 | tf_op jit(solution)/shard_map/ppermute | solution.py:23
  24.5 54.4 %collective-permute-start.8 = (bf16[48,2048]{1,0:T(8,128)(2,1)}, bf16[48,2048]{1,0:T(8,128)(2,1)}, u32[]{:S(2)}, u32[]{:S(2)}) collective-permute-start(bf16[48,2048]{1,0:T(8,128)(2,1)} %get-tuple-element.145), channel_id=1, source_target_pairs={{0,24},{4,28},{8,16},{12,20},{16,8},{20,12},{24,0},{28,4},{1,25},{... | collective-permute-start | bytes 589832 | tf_op jit(solution)/shard_map/ppermute | solution.py:23
  28.1 50.8 %collective-permute-start.9 = (bf16[48,2048]{1,0:T(8,128)(2,1)}, bf16[48,2048]{1,0:T(8,128)(2,1)}, u32[]{:S(2)}, u32[]{:S(2)}) collective-permute-start(bf16[48,2048]{1,0:T(8,128)(2,1)} %get-tuple-element.146), channel_id=1, source_target_pairs={{0,28},{4,24},{8,20},{12,16},{16,12},{20,8},{24,4},{28,0},{1,29},{... | collective-permute-start | bytes 589832 | tf_op jit(solution)/shard_map/ppermute | solution.py:23
  49.3 21.2 %collective-permute-start.6 = (bf16[192,2048]{1,0:T(8,128)(2,1)S(1)}, bf16[192,2048]{1,0:T(8,128)(2,1)S(1)}, u32[]{:S(2)}, u32[]{:S(2)}) collective-permute-start(bf16[192,2048]{1,0:T(8,128)(2,1)S(1)} %constant_dynamic-update-slice_fusion.refs_0_), channel_id=1, source_target_pairs={{0,1},{1,0},{2,3},{3,2},{4,5},{5,4},{6,7},{7,6},{8,9},{9,8},{10,11... | collective-permute-start | bytes 2359304 | tf_op jit(solution)/shard_map/ppermute | solution.py:23
  60.4 10.1 %collective-permute-start.7 = (bf16[192,2048]{1,0:T(8,128)(2,1)S(1)}, bf16[192,2048]{1,0:T(8,128)(2,1)S(1)}, u32[]{:S(2)}, u32[]{:S(2)}) collective-permute-start(bf16[192,2048]{1,0:T(8,128)(2,1)S(1)} %collective-permute-done.5.refs_2_), channel_id=1, source_target_pairs={{0,1},{1,0},{2,3},{3,2},{4,5},{5,4},{6,7},{7,6},{8,9},{9,8},{10,11... | collective-permute-start | bytes 2359304 | tf_op jit(solution)/shard_map/ppermute | solution.py:23
  60.6 18.3 %collective-permute-start.10 = (bf16[96,2048]{1,0:T(8,128)(2,1)S(1)}, bf16[96,2048]{1,0:T(8,128)(2,1)}, u32[]{:S(2)}, u32[]{:S(2)}) collective-permute-start(bf16[96,2048]{1,0:T(8,128)(2,1)S(1)} %constant_dynamic-update-slice_fusion.4.refs_0_), channel_id=1, source_target_pairs={{0,2},{1,3},{2,0},{3,1},{4,6},{5,7},{6,4},{7,5},{8,10},{9,11},{10,... | collective-permute-start | bytes 1179656 | tf_op jit(solution)/shard_map/ppermute | solution.py:23
  88.4 11.9 %collective-permute-start.17 = (bf16[96,2048]{1,0:T(8,128)(2,1)S(1)}, bf16[96,2048]{1,0:T(8,128)(2,1)S(1)}, u32[]{:S(2)}, u32[]{:S(2)}) collective-permute-start(bf16[96,2048]{1,0:T(8,128)(2,1)S(1)} %constant_dynamic-update-slice_fusion.6.refs_0_), channel_id=1, source_target_pairs={{0,2},{1,3},{2,0},{3,1},{4,6},{5,7},{6,4},{7,5},{8,10},{9,11},{10,... | collective-permute-start | bytes 1179656 | tf_op jit(solution)/shard_map/ppermute | solution.py:23
  89.1 11.2 %collective-permute-start.13 = (bf16[96,2048]{1,0:T(8,128)(2,1)S(1)}, bf16[96,2048]{1,0:T(8,128)(2,1)S(1)}, u32[]{:S(2)}, u32[]{:S(2)}) collective-permute-start(bf16[96,2048]{1,0:T(8,128)(2,1)S(1)} %get-tuple-element.153), channel_id=1, source_target_pairs={{0,1},{1,0},{2,3},{3,2},{4,5},{5,4},{6,7},{7,6},{8,9},{9,8},{10,11... | collective-permute-start | bytes 1179656 | tf_op jit(solution)/shard_map/ppermute | solution.py:23
  89.2 26.4 %collective-permute-start.23 = (bf16[192,2048]{1,0:T(8,128)(2,1)S(1)}, bf16[192,2048]{1,0:T(8,128)(2,1)S(1)}, u32[]{:S(2)}, u32[]{:S(2)}) collective-permute-start(bf16[192,2048]{1,0:T(8,128)(2,1)S(1)} %get-tuple-element.173), channel_id=1, source_target_pairs={{0,1},{1,0},{2,3},{3,2},{4,5},{5,4},{6,7},{7,6},{8,9},{9,8},{10,11... | collective-permute-start | bytes 2359304 | tf_op jit(solution)/shard_map/ppermute | solution.py:23
  90.1 18.1 %collective-permute-start.15 = (bf16[96,2048]{1,0:T(8,128)(2,1)S(1)}, bf16[96,2048]{1,0:T(8,128)(2,1)S(1)}, u32[]{:S(2)}, u32[]{:S(2)}) collective-permute-start(bf16[96,2048]{1,0:T(8,128)(2,1)S(1)} %add_convert_fusion.5), channel_id=1, source_target_pairs={{0,2},{1,3},{2,0},{3,1},{4,6},{5,7},{6,4},{7,5},{8,10},{9,11},{10,... | collective-permute-start | bytes 1179656 | tf_op jit(solution)/shard_map/ppermute | solution.py:23
  91.1 17.2 %collective-permute-start.16 = (bf16[96,2048]{1,0:T(8,128)(2,1)S(1)}, bf16[96,2048]{1,0:T(8,128)(2,1)S(1)}, u32[]{:S(2)}, u32[]{:S(2)}) collective-permute-start(bf16[96,2048]{1,0:T(8,128)(2,1)S(1)} %constant_dynamic-update-slice_fusion.6.refs_0_), channel_id=1, source_target_pairs={{0,1},{1,0},{2,3},{3,2},{4,5},{5,4},{6,7},{7,6},{8,9},{9,8},{10,11... | collective-permute-start | bytes 1179656 | tf_op jit(solution)/shard_map/ppermute | solution.py:23
  100.4 17.1 %collective-permute-start.22 = (bf16[192,2048]{1,0:T(8,128)(2,1)S(1)}, bf16[192,2048]{1,0:T(8,128)(2,1)S(1)}, u32[]{:S(2)}, u32[]{:S(2)}) collective-permute-start(bf16[192,2048]{1,0:T(8,128)(2,1)S(1)} %get-tuple-element.171), channel_id=1, source_target_pairs={{0,1},{1,0},{2,3},{3,2},{4,5},{5,4},{6,7},{7,6},{8,9},{9,8},{10,11... | collective-permute-start | bytes 2359304 | tf_op jit(solution)/shard_map/ppermute | solution.py:23
  117.5 42.7 %collective-permute-start.24 = (bf16[192,2048]{1,0:T(8,128)(2,1)S(1)}, bf16[192,2048]{1,0:T(8,128)(2,1)S(1)}, u32[]{:S(2)}, u32[]{:S(2)}) collective-permute-start(bf16[192,2048]{1,0:T(8,128)(2,1)S(1)} %add_convert_fusion.1), channel_id=1, source_target_pairs={{0,2},{1,3},{2,0},{3,1},{4,6},{5,7},{6,4},{7,5},{8,10},{9,11},{10,... | collective-permute-start | bytes 2359304 | tf_op jit(solution)/shard_map/ppermute | solution.py:23
  118.3 27.4 %collective-permute-start.21 = (bf16[96,2048]{1,0:T(8,128)(2,1)S(1)}, bf16[96,2048]{1,0:T(8,128)(2,1)S(1)}, u32[]{:S(2)}, u32[]{:S(2)}) collective-permute-start(bf16[96,2048]{1,0:T(8,128)(2,1)S(1)} %add_convert_fusion.4), channel_id=1, source_target_pairs={{0,2},{1,3},{2,0},{3,1},{4,6},{5,7},{6,4},{7,5},{8,10},{9,11},{10,... | collective-permute-start | bytes 1179656 | tf_op jit(solution)/shard_map/ppermute | solution.py:23
  119.6 42.7 %collective-permute-start.30 = (bf16[48,2048]{1,0:T(8,128)(2,1)S(1)}, bf16[48,2048]{1,0:T(8,128)(2,1)S(1)}, u32[]{:S(2)}, u32[]{:S(2)}) collective-permute-start(bf16[48,2048]{1,0:T(8,128)(2,1)S(1)} %get-tuple-element.156), channel_id=1, source_target_pairs={{0,16},{4,20},{8,24},{12,28},{16,0},{20,4},{24,8},{28,12},{1,17},{... | collective-permute-start | bytes 589832 | tf_op jit(solution)/shard_map/ppermute | solution.py:23
  122.2 40.1 %collective-permute-start.31 = (bf16[48,2048]{1,0:T(8,128)(2,1)S(1)}, bf16[48,2048]{1,0:T(8,128)(2,1)S(1)}, u32[]{:S(2)}, u32[]{:S(2)}) collective-permute-start(bf16[48,2048]{1,0:T(8,128)(2,1)S(1)} %get-tuple-element.157), channel_id=1, source_target_pairs={{0,20},{4,16},{8,28},{12,24},{16,4},{20,0},{24,12},{28,8},{1,21},{... | collective-permute-start | bytes 589832 | tf_op jit(solution)/shard_map/ppermute | solution.py:23
  124.7 37.0 %collective-permute-start.26 = (f32[16,128]{1,0:T(8,128)S(1)}, f32[16,128]{1,0:T(8,128)S(1)}, u32[]{:S(2)}, u32[]{:S(2)}) collective-permute-start(f32[16,128]{1,0:T(8,128)S(1)} %add.33), channel_id=1, source_target_pairs={{0,2},{1,3},{2,0},{3,1},{4,6},{5,7},{6,4},{7,5},{8,10},{9,11},{10,... | collective-permute-start | bytes 24584 | tf_op jit(solution)/shard_map/ppermute | solution.py:23
  145.8 26.8 %collective-permute-start.32 = (bf16[48,2048]{1,0:T(8,128)(2,1)S(1)}, bf16[48,2048]{1,0:T(8,128)(2,1)S(1)}, u32[]{:S(2)}, u32[]{:S(2)}) collective-permute-start(bf16[48,2048]{1,0:T(8,128)(2,1)S(1)} %get-tuple-element.167), channel_id=1, source_target_pairs={{0,24},{4,28},{8,16},{12,20},{16,8},{20,12},{24,0},{28,4},{1,25},{... | collective-permute-start | bytes 589832 | tf_op jit(solution)/shard_map/ppermute | solution.py:23
  160.2 12.4 %collective-permute-start.33 = (bf16[48,2048]{1,0:T(8,128)(2,1)S(1)}, bf16[48,2048]{1,0:T(8,128)(2,1)S(1)}, u32[]{:S(2)}, u32[]{:S(2)}) collective-permute-start(bf16[48,2048]{1,0:T(8,128)(2,1)S(1)} %get-tuple-element.168), channel_id=1, source_target_pairs={{0,28},{4,24},{8,20},{12,16},{16,12},{20,8},{24,4},{28,0},{1,29},{... | collective-permute-start | bytes 589832 | tf_op jit(solution)/shard_map/ppermute | solution.py:23
  161.7 10.9 %collective-permute-start.27 = (bf16[48,2048]{1,0:T(8,128)(2,1)S(1)}, bf16[48,2048]{1,0:T(8,128)(2,1)S(1)}, u32[]{:S(2)}, u32[]{:S(2)}) collective-permute-start(bf16[48,2048]{1,0:T(8,128)(2,1)S(1)} %get-tuple-element.185), channel_id=1, source_target_pairs={{0,4},{4,0},{8,12},{12,8},{16,20},{20,16},{24,28},{28,24},{1,5},{5... | collective-permute-start | bytes 589832 | tf_op jit(solution)/shard_map/ppermute | solution.py:23
  162.3 10.8 %collective-permute-start.28 = (bf16[48,2048]{1,0:T(8,128)(2,1)S(1)}, bf16[48,2048]{1,0:T(8,128)(2,1)S(1)}, u32[]{:S(2)}, u32[]{:S(2)}) collective-permute-start(bf16[48,2048]{1,0:T(8,128)(2,1)S(1)} %get-tuple-element.186), channel_id=1, source_target_pairs={{0,8},{4,12},{8,0},{12,4},{16,24},{20,28},{24,16},{28,20},{1,9},{5... | collective-permute-start | bytes 589832 | tf_op jit(solution)/shard_map/ppermute | solution.py:23
  162.3 14.6 %collective-permute-start.29 = (bf16[48,2048]{1,0:T(8,128)(2,1)S(1)}, bf16[48,2048]{1,0:T(8,128)(2,1)S(1)}, u32[]{:S(2)}, u32[]{:S(2)}) collective-permute-start(bf16[48,2048]{1,0:T(8,128)(2,1)S(1)} %get-tuple-element.187), channel_id=1, source_target_pairs={{0,12},{4,8},{8,4},{12,0},{16,28},{20,24},{24,20},{28,16},{1,13},{... | collective-permute-start | bytes 589832 | tf_op jit(solution)/shard_map/ppermute | solution.py:23
  179.1 11.5 %collective-permute-start.40 = (bf16[48,2048]{1,0:T(8,128)(2,1)S(1)}, bf16[48,2048]{1,0:T(8,128)(2,1)S(1)}, u32[]{:S(2)}, u32[]{:S(2)}) collective-permute-start(bf16[48,2048]{1,0:T(8,128)(2,1)S(1)} %get-tuple-element.198), channel_id=1, source_target_pairs={{0,12},{4,8},{8,4},{12,0},{16,28},{20,24},{24,20},{28,16},{1,13},{... | collective-permute-start | bytes 589832 | tf_op jit(solution)/shard_map/ppermute | solution.py:23
  190.6 18.8 %collective-permute-start.42 = (bf16[192,2048]{1,0:T(8,128)(2,1)S(1)}, bf16[192,2048]{1,0:T(8,128)(2,1)S(1)}, u32[]{:S(2)}, u32[]{:S(2)}) collective-permute-start(bf16[192,2048]{1,0:T(8,128)(2,1)S(1)} %constant_dynamic-update-slice_fusion.10.refs_0_), channel_id=1, source_target_pairs={{0,2},{1,3},{2,0},{3,1},{4,6},{5,7},{6,4},{7,5},{8,10},{9,11},{10,... | collective-permute-start | bytes 2359304 | tf_op jit(solution)/shard_map/ppermute | solution.py:23
  191.3 14.6 %collective-permute-start.36 = (bf16[48,2048]{1,0:T(8,128)(2,1)S(1)}, bf16[48,2048]{1,0:T(8,128)(2,1)S(1)}, u32[]{:S(2)}, u32[]{:S(2)}) collective-permute-start(bf16[48,2048]{1,0:T(8,128)(2,1)S(1)} %get-tuple-element.190), channel_id=1, source_target_pairs={{0,16},{4,20},{8,24},{12,28},{16,0},{20,4},{24,8},{28,12},{1,17},{... | collective-permute-start | bytes 589832 | tf_op jit(solution)/shard_map/ppermute | solution.py:23
  191.3 18.1 %collective-permute-start.37 = (bf16[48,2048]{1,0:T(8,128)(2,1)S(1)}, bf16[48,2048]{1,0:T(8,128)(2,1)S(1)}, u32[]{:S(2)}, u32[]{:S(2)}) collective-permute-start(bf16[48,2048]{1,0:T(8,128)(2,1)S(1)} %get-tuple-element.191), channel_id=1, source_target_pairs={{0,20},{4,16},{8,28},{12,24},{16,4},{20,0},{24,12},{28,8},{1,21},{... | collective-permute-start | bytes 589832 | tf_op jit(solution)/shard_map/ppermute | solution.py:23
  193.9 22.3 %collective-permute-start.41 = (bf16[192,2048]{1,0:T(8,128)(2,1)S(1)}, bf16[192,2048]{1,0:T(8,128)(2,1)S(1)}, u32[]{:S(2)}, u32[]{:S(2)}) collective-permute-start(bf16[192,2048]{1,0:T(8,128)(2,1)S(1)} %constant_dynamic-update-slice_fusion.10.refs_0_), channel_id=1, source_target_pairs={{0,1},{1,0},{2,3},{3,2},{4,5},{5,4},{6,7},{7,6},{8,9},{9,8},{10,11... | collective-permute-start | bytes 2359304 | tf_op jit(solution)/shard_map/ppermute | solution.py:23
  209.5 16.1 %collective-permute-start.46 = (bf16[96,2048]{1,0:T(8,128)(2,1)S(1)}, bf16[96,2048]{1,0:T(8,128)(2,1)S(1)}, u32[]{:S(2)}, u32[]{:S(2)}) collective-permute-start(bf16[96,2048]{1,0:T(8,128)(2,1)S(1)} %constant_dynamic-update-slice_fusion.8.refs_0_), channel_id=1, source_target_pairs={{0,2},{1,3},{2,0},{3,1},{4,6},{5,7},{6,4},{7,5},{8,10},{9,11},{10,... | collective-permute-start | bytes 1179656 | tf_op jit(solution)/shard_map/ppermute | solution.py:23
  211.0 13.7 %collective-permute-start.44 = (bf16[48,2048]{1,0:T(8,128)(2,1)S(1)}, bf16[48,2048]{1,0:T(8,128)(2,1)S(1)}, u32[]{:S(2)}, u32[]{:S(2)}) collective-permute-start(bf16[48,2048]{1,0:T(8,128)(2,1)S(1)} %get-tuple-element.207), channel_id=1, source_target_pairs={{0,24},{4,28},{8,16},{12,20},{16,8},{20,12},{24,0},{28,4},{1,25},{... | collective-permute-start | bytes 589832 | tf_op jit(solution)/shard_map/ppermute | solution.py:23
  211.3 14.3 %collective-permute-start.45 = (bf16[48,2048]{1,0:T(8,128)(2,1)S(1)}, bf16[48,2048]{1,0:T(8,128)(2,1)S(1)}, u32[]{:S(2)}, u32[]{:S(2)}) collective-permute-start(bf16[48,2048]{1,0:T(8,128)(2,1)S(1)} %get-tuple-element.208), channel_id=1, source_target_pairs={{0,28},{4,24},{8,20},{12,16},{16,12},{20,8},{24,4},{28,0},{1,29},{... | collective-permute-start | bytes 589832 | tf_op jit(solution)/shard_map/ppermute | solution.py:23
  234.7 11.9 %collective-permute-start.55 = (bf16[96,2048]{1,0:T(8,128)(2,1)S(1)}, bf16[96,2048]{1,0:T(8,128)(2,1)S(1)}, u32[]{:S(2)}, u32[]{:S(2)}) collective-permute-start(bf16[96,2048]{1,0:T(8,128)(2,1)S(1)} %constant_dynamic-update-slice_fusion.14.refs_0_), channel_id=1, source_target_pairs={{0,2},{1,3},{2,0},{3,1},{4,6},{5,7},{6,4},{7,5},{8,10},{9,11},{10,... | collective-permute-start | bytes 1179656 | tf_op jit(solution)/shard_map/ppermute | solution.py:23
  235.3 11.4 %collective-permute-start.51 = (bf16[96,2048]{1,0:T(8,128)(2,1)S(1)}, bf16[96,2048]{1,0:T(8,128)(2,1)S(1)}, u32[]{:S(2)}, u32[]{:S(2)}) collective-permute-start(bf16[96,2048]{1,0:T(8,128)(2,1)S(1)} %get-tuple-element.215), channel_id=1, source_target_pairs={{0,1},{1,0},{2,3},{3,2},{4,5},{5,4},{6,7},{7,6},{8,9},{9,8},{10,11... | collective-permute-start | bytes 1179656 | tf_op jit(solution)/shard_map/ppermute | solution.py:23
  235.4 26.8 %collective-permute-start.50 = (bf16[192,2048]{1,0:T(8,128)(2,1)S(1)}, bf16[192,2048]{1,0:T(8,128)(2,1)S(1)}, u32[]{:S(2)}, u32[]{:S(2)}) collective-permute-start(bf16[192,2048]{1,0:T(8,128)(2,1)S(1)} %get-tuple-element.221), channel_id=1, source_target_pairs={{0,1},{1,0},{2,3},{3,2},{4,5},{5,4},{6,7},{7,6},{8,9},{9,8},{10,11... | collective-permute-start | bytes 2359304 | tf_op jit(solution)/shard_map/ppermute | solution.py:23
  236.4 18.1 %collective-permute-start.53 = (bf16[96,2048]{1,0:T(8,128)(2,1)S(1)}, bf16[96,2048]{1,0:T(8,128)(2,1)S(1)}, u32[]{:S(2)}, u32[]{:S(2)}) collective-permute-start(bf16[96,2048]{1,0:T(8,128)(2,1)S(1)} %add_convert_fusion.3), channel_id=1, source_target_pairs={{0,2},{1,3},{2,0},{3,1},{4,6},{5,7},{6,4},{7,5},{8,10},{9,11},{10,... | collective-permute-start | bytes 1179656 | tf_op jit(solution)/shard_map/ppermute | solution.py:23
  237.4 17.2 %collective-permute-start.54 = (bf16[96,2048]{1,0:T(8,128)(2,1)S(1)}, bf16[96,2048]{1,0:T(8,128)(2,1)S(1)}, u32[]{:S(2)}, u32[]{:S(2)}) collective-permute-start(bf16[96,2048]{1,0:T(8,128)(2,1)S(1)} %constant_dynamic-update-slice_fusion.14.refs_0_), channel_id=1, source_target_pairs={{0,1},{1,0},{2,3},{3,2},{4,5},{5,4},{6,7},{7,6},{8,9},{9,8},{10,11... | collective-permute-start | bytes 1179656 | tf_op jit(solution)/shard_map/ppermute | solution.py:23
  246.6 17.3 %collective-permute-start.49 = (bf16[192,2048]{1,0:T(8,128)(2,1)S(1)}, bf16[192,2048]{1,0:T(8,128)(2,1)S(1)}, u32[]{:S(2)}, u32[]{:S(2)}) collective-permute-start(bf16[192,2048]{1,0:T(8,128)(2,1)S(1)} %get-tuple-element.219), channel_id=1, source_target_pairs={{0,1},{1,0},{2,3},{3,2},{4,5},{5,4},{6,7},{7,6},{8,9},{9,8},{10,11... | collective-permute-start | bytes 2359304 | tf_op jit(solution)/shard_map/ppermute | solution.py:23
  264.0 28.7 %collective-permute-start.59 = (bf16[192,2048]{1,0:T(8,128)(2,1)S(1)}, bf16[192,2048]{1,0:T(8,128)(2,1)S(1)}, u32[]{:S(2)}, u32[]{:S(2)}) collective-permute-start(bf16[192,2048]{1,0:T(8,128)(2,1)S(1)} %add_convert_fusion), channel_id=1, source_target_pairs={{0,2},{1,3},{2,0},{3,1},{4,6},{5,7},{6,4},{7,5},{8,10},{9,11},{10,... | collective-permute-start | bytes 2359304 | tf_op jit(solution)/shard_map/ppermute | solution.py:23
  264.6 27.5 %collective-permute-start.60 = (bf16[96,2048]{1,0:T(8,128)(2,1)S(1)}, bf16[96,2048]{1,0:T(8,128)(2,1)S(1)}, u32[]{:S(2)}, u32[]{:S(2)}) collective-permute-start(bf16[96,2048]{1,0:T(8,128)(2,1)S(1)} %add_convert_fusion.2), channel_id=1, source_target_pairs={{0,2},{1,3},{2,0},{3,1},{4,6},{5,7},{6,4},{7,5},{8,10},{9,11},{10,... | collective-permute-start | bytes 1179656 | tf_op jit(solution)/shard_map/ppermute | solution.py:23
  266.1 31.9 %collective-permute-start.64 = (bf16[48,2048]{1,0:T(8,128)(2,1)S(1)}, bf16[48,2048]{1,0:T(8,128)(2,1)S(1)}, u32[]{:S(2)}, u32[]{:S(2)}) collective-permute-start(bf16[48,2048]{1,0:T(8,128)(2,1)S(1)} %get-tuple-element.222), channel_id=1, source_target_pairs={{0,16},{4,20},{8,24},{12,28},{16,0},{20,4},{24,8},{28,12},{1,17},{... | collective-permute-start | bytes 589832 | tf_op jit(solution)/shard_map/ppermute | solution.py:23
  270.8 29.2 %collective-permute-start.65 = (bf16[48,2048]{1,0:T(8,128)(2,1)S(1)}, bf16[48,2048]{1,0:T(8,128)(2,1)S(1)}, u32[]{:S(2)}, u32[]{:S(2)}) collective-permute-start(bf16[48,2048]{1,0:T(8,128)(2,1)S(1)} %get-tuple-element.223), channel_id=1, source_target_pairs={{0,20},{4,16},{8,28},{12,24},{16,4},{20,0},{24,12},{28,8},{1,21},{... | collective-permute-start | bytes 589832 | tf_op jit(solution)/shard_map/ppermute | solution.py:23
  273.3 22.6 %collective-permute-start.35 = (f32[16,128]{1,0:T(8,128)S(1)}, f32[16,128]{1,0:T(8,128)S(1)}, u32[]{:S(2)}, u32[]{:S(2)}) collective-permute-start(f32[16,128]{1,0:T(8,128)S(1)} %add.35), channel_id=1, source_target_pairs={{0,2},{1,3},{2,0},{3,1},{4,6},{5,7},{6,4},{7,5},{8,10},{9,11},{10,... | collective-permute-start | bytes 24584 | tf_op jit(solution)/shard_map/ppermute | solution.py:23
  292.3 9.9 %collective-permute-start.66 = (bf16[48,2048]{1,0:T(8,128)(2,1)S(1)}, bf16[48,2048]{1,0:T(8,128)(2,1)S(1)}, u32[]{:S(2)}, u32[]{:S(2)}) collective-permute-start(bf16[48,2048]{1,0:T(8,128)(2,1)S(1)} %get-tuple-element.232), channel_id=1, source_target_pairs={{0,24},{4,28},{8,16},{12,20},{16,8},{20,12},{24,0},{28,4},{1,25},{... | collective-permute-start | bytes 589832 | tf_op jit(solution)/shard_map/ppermute | solution.py:23
  292.7 12.4 %collective-permute-start.67 = (bf16[48,2048]{1,0:T(8,128)(2,1)S(1)}, bf16[48,2048]{1,0:T(8,128)(2,1)S(1)}, u32[]{:S(2)}, u32[]{:S(2)}) collective-permute-start(bf16[48,2048]{1,0:T(8,128)(2,1)S(1)} %get-tuple-element.233), channel_id=1, source_target_pairs={{0,28},{4,24},{8,20},{12,16},{16,12},{20,8},{24,4},{28,0},{1,29},{... | collective-permute-start | bytes 589832 | tf_op jit(solution)/shard_map/ppermute | solution.py:23
  296.0 10.0 %collective-permute-start.61 = (bf16[48,2048]{1,0:T(8,128)(2,1)S(1)}, bf16[48,2048]{1,0:T(8,128)(2,1)S(1)}, u32[]{:S(2)}, u32[]{:S(2)}) collective-permute-start(bf16[48,2048]{1,0:T(8,128)(2,1)S(1)} %get-tuple-element.238), channel_id=1, source_target_pairs={{0,4},{4,0},{8,12},{12,8},{16,20},{20,16},{24,28},{28,24},{1,5},{5... | collective-permute-start | bytes 589832 | tf_op jit(solution)/shard_map/ppermute | solution.py:23
  298.0 10.8 %collective-permute-start.62 = (bf16[48,2048]{1,0:T(8,128)(2,1)S(1)}, bf16[48,2048]{1,0:T(8,128)(2,1)S(1)}, u32[]{:S(2)}, u32[]{:S(2)}) collective-permute-start(bf16[48,2048]{1,0:T(8,128)(2,1)S(1)} %get-tuple-element.239), channel_id=1, source_target_pairs={{0,8},{4,12},{8,0},{12,4},{16,24},{20,28},{24,16},{28,20},{1,9},{5... | collective-permute-start | bytes 589832 | tf_op jit(solution)/shard_map/ppermute | solution.py:23
  300.0 12.5 %collective-permute-start.63 = (bf16[48,2048]{1,0:T(8,128)(2,1)S(1)}, bf16[48,2048]{1,0:T(8,128)(2,1)S(1)}, u32[]{:S(2)}, u32[]{:S(2)}) collective-permute-start(bf16[48,2048]{1,0:T(8,128)(2,1)S(1)} %get-tuple-element.240), channel_id=1, source_target_pairs={{0,12},{4,8},{8,4},{12,0},{16,28},{20,24},{24,20},{28,16},{1,13},{... | collective-permute-start | bytes 589832 | tf_op jit(solution)/shard_map/ppermute | solution.py:23
  (34 other events, 281.4 us)
